TPU v7x, 32 devices: a whole 2x2x4 slice. The times are simulated.
32 devices in a mesh: segment: 2 (over y), tile: 16 (over z, x, core).
Axes of the slice: x: 2, y: 2, z: 4, core: 2. Of those that a mesh axis runs over, the one named last changes fastest.
Arguments:
- coarse: bfloat16 [2, 8, 64, 128], P(None, None, 'tile'), may hold values from -6 to 6
- noise_draw: float32 [2, 4, 128, 128], P(None, None, 'tile'), may hold values from -6 to 6
- reg_in: bfloat16 [192, 72], replicated, may hold values from -0.75 to 0.75
- reg_mid: bfloat16 [2, 192, 1728], replicated, may hold values from -0.15625 to 0.15625
- reg_out: bfloat16 [4, 192], replicated, may hold values from -0.4375 to 0.4375
- diff_in: bfloat16 [256, 144], replicated, may hold values from -0.5 to 0.5
- diff_skip: bfloat16 [256, 192], replicated, may hold values from -0.4375 to 0.4375
- diff_mid: bfloat16 [256, 2304], replicated, may hold values from -0.125 to 0.125
- diff_out: bfloat16 [4, 256], replicated, may hold values from -0.375 to 0.375
- noise_embed: float32 [256], replicated, may hold values from -5 to 5
Outputs:
- fields: float32 [2, 2, 4, 64, 128], P('segment', None, None, 'tile')
All inputs are finite; a program needn't handle non-finite values.
Results may differ from a plain program's by a relative error of at most 0.004.
Values may be sent and summed in bfloat16 or wider, within the bound.
No kernel may reach another device: no remote copies, remote signals or barrier semaphores. Data moves between devices by JAX's collectives and lax.ppermute only.
A program may use at most 64 MiB of HBM per device.

v0:
```python
import math

import jax
import jax.numpy as jnp
from jax import lax
from jax.experimental import pallas as pl
from jax.experimental.pallas import tpu as pltpu
from jax.sharding import PartitionSpec as P

GROUPS = 32
LANES = 128
BAND = 4
MARGIN = 2
ROWS = BAND + 2 * MARGIN

sigma_high = 4.0
sigma_low = 0.5
sigma_data = 0.5

F32 = jnp.float32
BF16 = jnp.bfloat16


def lanes(first, count=1):
    return slice(first * LANES, (first + count) * LANES)


def lane_ids(shape):
    return lax.broadcasted_iota(jnp.int32, shape, len(shape) - 1)


def col_shifts(chunk):
    lane = lane_ids(chunk.shape)
    zero = jnp.zeros_like(chunk)
    before = jnp.where(lane == 0, zero, pltpu.roll(chunk, 1, 1))
    after = jnp.where(lane == LANES - 1, zero, pltpu.roll(chunk, LANES - 1, 1))
    return before, chunk, after


def store_row(taps_ref, row, chunk):
    channels = chunk.shape[0]
    for b, piece in enumerate(col_shifts(chunk)):
        taps_ref[b * channels : (b + 1) * channels, lanes(row + 1)] = piece.astype(BF16)


def clear_edges(taps_ref):
    zero = jnp.zeros((taps_ref.shape[0], LANES), BF16)
    taps_ref[:, lanes(0)] = zero
    taps_ref[:, lanes(ROWS + 1)] = zero


def group_total(part):
    channels = part.shape[0]
    size = channels // GROUPS
    if size == 8:
        total = jnp.sum(part.reshape(GROUPS, 8, LANES), axis=(1, 2), keepdims=True)
        return jnp.broadcast_to(total, (GROUPS, 8, LANES)).reshape(channels, LANES)
    blocks = channels // 24
    tiles = part.reshape(blocks, 3, 8, LANES)
    row = lax.broadcasted_iota(jnp.int32, (blocks, 8, LANES), 1)
    v0, v1, v2 = tiles[:, 0], tiles[:, 1], tiles[:, 2]
    zero = jnp.zeros_like(v0)
    sums = (
        jnp.where(row < 6, v0, zero),
        jnp.where(row >= 6, v0, zero) + jnp.where(row < 4, v1, zero),
        jnp.where(row >= 4, v1, zero) + jnp.where(row < 2, v2, zero),
        jnp.where(row >= 2, v2, zero),
    )
    t0, t1, t2, t3 = (
        jnp.broadcast_to(jnp.sum(s, axis=(1, 2), keepdims=True), (blocks, 8, LANES)) for s in sums
    )
    m0 = jnp.where(row < 6, t0, t1)
    m1 = jnp.where(row < 4, t1, t2)
    m2 = jnp.where(row < 2, t2, t3)
    return jnp.stack([m0, m1, m2], axis=1).reshape(channels, LANES)


def norm_scales(hidden_ref):
    channels = hidden_ref.shape[0]
    share = 1.0 / (channels // GROUPS * ROWS * LANES)
    total = hidden_ref[:, lanes(0)]
    for r in range(1, ROWS):
        total = total + hidden_ref[:, lanes(r)]
    centre = group_total(total) * share
    square = jnp.zeros_like(centre)
    for r in range(ROWS):
        away = hidden_ref[:, lanes(r)] - centre
        square = square + away * away
    half = 0.5 * lax.rsqrt(group_total(square) * share + 1e-5)
    return centre, half


def act_row(hidden_ref, row, scales):
    centre, half = scales
    v = (hidden_ref[:, lanes(row)] - centre) * half
    return v + v * jnp.tanh(v)


def conv_rows(weight, taps_ref, first, count):
    depth = taps_ref.shape[0]
    out = None
    for a in range(3):
        term = jnp.dot(
            weight(a * depth, depth), taps_ref[:, lanes(first + a, count)], preferred_element_type=F32
        )
        out = term if out is None else out + term
    return out


def input_taps(rows, out_ref):
    shifted = [col_shifts(row) for row in rows]
    blank = jnp.zeros_like(rows[0])
    for i in range(ROWS):
        pieces = []
        for a in range(3):
            pieces.extend(shifted[i + a - 1] if 0 <= i + a - 1 < ROWS else [blank] * 3)
        out_ref[:, lanes(i)] = jnp.concatenate(pieces, axis=0).astype(BF16)


def place():
    tile = lax.axis_index("tile")
    count = lax.axis_size("tile")
    return lax.rem(tile, 2) == 0, tile == 0, tile == count - 1


def regress_kernel(
    coarse_ref, pair_ref, next_ref, far_ref, reg_in_ref, reg_mid_ref, reg_out_ref,
    skip_ref, reg_ref, send_skip_ref, send_reg_ref, outer_skip_ref, outer_reg_ref,
    taps_in, hidden_a, hidden_b, taps_a, taps_b,
):
    even, first, last = place()
    sample = lax.axis_index("segment")

    def rows_of(ref):
        block = ref[sample].astype(F32)
        return [block[:, r, :] for r in range(BAND)]

    own, pair, across, far = (rows_of(ref) for ref in (coarse_ref, pair_ref, next_ref, far_ref))
    window = [jnp.where(even, far[2 + i], pair[2 + i]) for i in range(2)]
    window += [jnp.where(even, across[i], own[i]) for i in range(4)]
    window += [jnp.where(even, own[i], across[i]) for i in range(4)]
    window += [jnp.where(even, pair[i], far[i]) for i in range(2)]
    no_low = jnp.logical_and(even, first)
    no_high = jnp.logical_and(jnp.logical_not(even), last)
    window = [
        jnp.where(no_low if i < 6 else no_high, jnp.zeros_like(w), w) for i, w in enumerate(window)
    ]
    rows_a = [jnp.where(even, window[i + 4], window[i]) for i in range(ROWS)]
    rows_b = [jnp.where(even, window[i], window[i + 4]) for i in range(ROWS)]
    for rows, hidden, taps in ((rows_a, hidden_a, taps_a), (rows_b, hidden_b, taps_b)):
        clear_edges(taps)
        input_taps(rows, taps_in)
        hidden[...] = jnp.dot(reg_in_ref[...], taps_in[...], preferred_element_type=F32)

    step = 2
    for block in range(reg_mid_ref.shape[0]):
        for hidden, taps in ((hidden_a, taps_a), (hidden_b, taps_b)):
            scales = norm_scales(hidden)
            for r in range(ROWS):
                store_row(taps, r, act_row(hidden, r, scales))
            for r in range(0, ROWS, step):
                hidden[:, lanes(r, step)] += conv_rows(
                    lambda at, depth: reg_mid_ref[block, :, at : at + depth], taps, r, step
                )

    scales = norm_scales(hidden_a)
    for r in range(ROWS):
        act = act_row(hidden_a, r, scales).astype(BF16)
        reg_ref[:, lanes(r)] = jnp.dot(reg_out_ref[...], act, preferred_element_type=F32)
    for i in range(BAND):
        skip_ref[:, lanes(i)] = hidden_a[:, lanes(MARGIN + i)].astype(BF16)
        send_reg_ref[:, lanes(i)] = jnp.where(even, reg_ref[:, lanes(4 + i)], reg_ref[:, lanes(i)])
    for i in range(MARGIN):
        send_skip_ref[:, lanes(i)] = jnp.where(
            even, hidden_a[:, lanes(4 + i)], hidden_a[:, lanes(2 + i)]
        ).astype(BF16)
        outer_skip_ref[:, lanes(i)] = jnp.where(
            even, hidden_b[:, lanes(4 + i)], hidden_b[:, lanes(2 + i)]
        ).astype(BF16)
    centre, half = norm_scales(hidden_b)
    for i in range(BAND):
        v = (jnp.where(even, hidden_b[:, lanes(4 + i)], hidden_b[:, lanes(i)]) - centre) * half
        act = (v + v * jnp.tanh(v)).astype(BF16)
        outer_reg_ref[:, lanes(i)] = jnp.dot(reg_out_ref[...], act, preferred_element_type=F32)


def denoise_kernel(
    coarse_ref, pair_ref, next_ref, noise_ref, skip_ref, reg_ref, pair_skip_ref, pair_reg_ref,
    outer_skip_ref, outer_reg_ref, diff_in_ref, diff_skip_ref, diff_mid_ref, diff_out_ref, embed_ref,
    mean_ref, band_ref, send_pair_ref, send_next_ref,
    taps_in, skips, base, hidden, taps,
):
    even, first, last = place()
    sample = lax.axis_index("segment")
    clear_edges(taps)

    def rows_of(ref):
        block = ref[sample].astype(F32)
        return [block[:, r, :] for r in range(block.shape[1])]

    own, pair, across = (rows_of(ref) for ref in (coarse_ref, pair_ref, next_ref))
    coarse = [jnp.where(even, across[2 + i], pair[2 + i]) for i in range(2)]
    coarse += own
    coarse += [jnp.where(even, pair[i], across[i]) for i in range(2)]
    reg = [reg_ref[:, lanes(r)] for r in range(ROWS)]
    up = [jnp.where(even, outer_reg_ref[:, lanes(i)], pair_reg_ref[:, lanes(i)]) for i in range(4)]
    down = [jnp.where(even, pair_reg_ref[:, lanes(i)], outer_reg_ref[:, lanes(i)]) for i in range(4)]
    mean = []
    for r in range(ROWS):
        both = 0.5 * (reg[r] + (up[r] if r < 4 else down[r - 4]))
        if r < MARGIN:
            mean.append(jnp.where(first, jnp.zeros_like(both), both))
        elif r < 4:
            mean.append(jnp.where(first, reg[r], both))
        elif r < MARGIN + BAND:
            mean.append(jnp.where(last, reg[r], both))
        else:
            mean.append(jnp.where(last, jnp.zeros_like(both), both))
    for i in range(BAND):
        mean_ref[:, lanes(i)] = mean[MARGIN + i]
    mean = [m.astype(BF16).astype(F32) for m in mean]
    for i in range(2):
        coarse[i] = jnp.where(first, jnp.zeros_like(coarse[i]), coarse[i])
        coarse[6 + i] = jnp.where(last, jnp.zeros_like(coarse[i]), coarse[6 + i])
        low = jnp.where(even, outer_skip_ref[:, lanes(i)], pair_skip_ref[:, lanes(i)])
        high = jnp.where(even, pair_skip_ref[:, lanes(i)], outer_skip_ref[:, lanes(i)])
        skips[:, lanes(i)] = jnp.where(first, jnp.zeros_like(low), low)
        skips[:, lanes(6 + i)] = jnp.where(last, jnp.zeros_like(high), high)
    skips[:, lanes(MARGIN, BAND)] = skip_ref[...]
    base[...] = jnp.dot(diff_skip_ref[...], skips[...], preferred_element_type=F32)

    channels = diff_mid_ref.shape[0]
    embed = jnp.broadcast_to(embed_ref[...], (LANES, channels)).T
    noise = rows_of(noise_ref)
    initial = [sigma_high * n for n in noise]
    step = 2

    def denoise(current, sigma_now):
        total_var = sigma_now * sigma_now + sigma_data * sigma_data
        input_scale = 1.0 / math.sqrt(total_var)
        skip_coef = sigma_data * sigma_data / total_var
        out_coef = sigma_now * sigma_data / math.sqrt(total_var)
        input_taps(
            [
                jnp.concatenate([input_scale * current[r], coarse[r], mean[r]], axis=0)
                for r in range(ROWS)
            ],
            taps_in,
        )
        shift = (math.log(sigma_now) / 4.0) * embed
        for r in range(0, ROWS, step):
            hidden[:, lanes(r, step)] = (
                jnp.dot(diff_in_ref[...], taps_in[:, lanes(r, step)], preferred_element_type=F32)
                + base[:, lanes(r, step)]
                + jnp.concatenate([shift] * step, axis=1)
            )
        scales = norm_scales(hidden)
        for r in range(ROWS):
            store_row(taps, r, act_row(hidden, r, scales))
        for r in range(0, ROWS, step):
            hidden[:, lanes(r, step)] += conv_rows(
                lambda at, depth: diff_mid_ref[:, at : at + depth], taps, r, step
            )
        scales = norm_scales(hidden)
        result = []
        for r in range(ROWS):
            act = act_row(hidden, r, scales).astype(BF16)
            out = jnp.dot(diff_out_ref[...], act, preferred_element_type=F32)
            result.append(skip_coef * current[r] + out_coef * out)
        return result

    denoised = denoise(initial, sigma_high)
    stepped = [
        x + (sigma_low - sigma_high) * (x - d) / sigma_high for x, d in zip(initial, denoised)
    ]
    final = denoise(stepped, sigma_low)
    for i in range(BAND):
        band_ref[:, lanes(i)] = final[MARGIN + i]
    for i in range(MARGIN):
        send_pair_ref[:, lanes(i)] = jnp.where(even, final[6 + i], final[i])
        send_next_ref[:, lanes(i)] = jnp.where(even, final[i], final[6 + i])


def average_kernel(mean_ref, band_ref, pair_ref, next_ref, own_ref, send_ref):
    even, first, last = place()
    lower = lax.axis_index("segment") == 0
    for i in range(BAND):
        here = band_ref[:, lanes(i)]
        mean = mean_ref[:, lanes(i)]
        j = i % MARGIN
        if i < MARGIN:
            other = jnp.where(even, next_ref[:, lanes(j)], pair_ref[:, lanes(j)])
            alone = first
        else:
            other = jnp.where(even, pair_ref[:, lanes(j)], next_ref[:, lanes(j)])
            alone = last
        value = jnp.where(alone, here, 0.5 * (here + other)) + mean.astype(BF16).astype(F32)
        own_ref[:, i, :] = jnp.where(lower, mean, value)
        send_ref[:, i, :] = jnp.where(lower, value, mean)


def output_kernel(own_ref, got_ref, out_ref):
    lower = lax.axis_index("segment") == 0
    own, got = own_ref[...], got_ref[...]
    out_ref[0, 0] = jnp.where(lower, own, got)
    out_ref[0, 1] = jnp.where(lower, got, own)


def call(kernel, name, outs, scratch=()):
    return pl.pallas_call(
        kernel,
        name=name,
        out_shape=[jax.ShapeDtypeStruct(shape, dtype) for shape, dtype in outs],
        scratch_shapes=[pltpu.VMEM(shape, dtype) for shape, dtype in scratch],
        compiler_params=pltpu.CompilerParams(vmem_limit_bytes=32 * 1024 * 1024),
    )


def shards(
    coarse, noise_draw, reg_in, reg_mid, reg_out, diff_in, diff_skip, diff_mid, diff_out, noise_embed
):
    tiles = lax.axis_size("tile")
    pairs = [(i, i ^ 1) for i in range(tiles)]
    nexts = [(i, (i - 1 if i % 2 == 0 else i + 1) % tiles) for i in range(tiles)]
    fars = [(i, (i + 2 if i % 2 == 0 else i - 2) % tiles) for i in range(tiles)]
    swap = [(0, 1), (1, 0)]
    width_r, width_d, fields = reg_in.shape[0], diff_in.shape[0], reg_out.shape[0]
    cells = ROWS * LANES

    pair_coarse = lax.ppermute(coarse, "tile", pairs)
    next_coarse = lax.ppermute(coarse, "tile", nexts)
    far_coarse = lax.ppermute(coarse, "tile", fars)
    skip, reg, send_skip, send_reg, outer_skip, outer_reg = call(
        regress_kernel,
        "regress",
        [
            ((width_r, BAND * LANES), BF16),
            ((fields, cells), F32),
            ((width_r, MARGIN * LANES), BF16),
            ((fields, BAND * LANES), F32),
            ((width_r, MARGIN * LANES), BF16),
            ((fields, BAND * LANES), F32),
        ],
        [
            ((reg_in.shape[1], cells), BF16),
            ((width_r, cells), F32),
            ((width_r, cells), F32),
            ((3 * width_r, cells + 2 * LANES), BF16),
            ((3 * width_r, cells + 2 * LANES), BF16),
        ],
    )(coarse, pair_coarse, next_coarse, far_coarse, reg_in, reg_mid, reg_out)
    pair_skip = lax.ppermute(send_skip, "tile", pairs)
    pair_reg = lax.ppermute(send_reg, "tile", pairs)
    mean, band, send_pair, send_next = call(
        denoise_kernel,
        "denoise",
        [
            ((fields, BAND * LANES), F32),
            ((fields, BAND * LANES), F32),
            ((fields, MARGIN * LANES), F32),
            ((fields, MARGIN * LANES), F32),
        ],
        [
            ((diff_in.shape[1], cells), BF16),
            ((width_r, cells), BF16),
            ((width_d, cells), F32),
            ((width_d, cells), F32),
            ((3 * width_d, cells + 2 * LANES), BF16),
        ],
    )(
        coarse, pair_coarse, next_coarse, noise_draw, skip, reg, pair_skip, pair_reg,
        outer_skip, outer_reg, diff_in, diff_skip, diff_mid, diff_out, noise_embed[None],
    )
    pair_band = lax.ppermute(send_pair, "tile", pairs)
    next_band = lax.ppermute(send_next, "tile", nexts)
    piece = ((fields, BAND, LANES), F32)
    own, send = call(average_kernel, "average", [piece, piece])(mean, band, pair_band, next_band)
    got = lax.ppermute(send, "segment", swap)
    (out,) = call(output_kernel, "output", [((1, 2, fields, BAND, LANES), F32)])(own, got)
    return out


def solution(mesh):
    return jax.shard_map(
        shards,
        mesh=mesh,
        in_specs=(P(None, None, "tile", None), P(None, None, "tile", None)) + (P(),) * 8,
        out_specs=P("segment", None, None, "tile", None),
        check_vma=False,
    )
```

profile of v0, /device:TPU:0, one launch (start us, length us, event | category | flops | bytes accessed | tf_op | source)
XLA Modules:
  0.0 38.6 jit_solution(5221963836361495215)
XLA Ops:
  0.0 0.5 %collective-permute-start = (bf16[2,8,4,128]{3,2,1,0:T(4,128)(2,1)}, bf16[2,8,4,128]{3,2,1,0:T(4,128)(2,1)S(1)}, u32[]{:S(2)}, u32[]{:S(2)}) collective-permute-start(bf16[2,8,4,128]{3,2,1,0:T(4,128)(2,1)} %coarse_ref.3), channel_id=1, source_target_pairs={{0,1},{1,0},{2,3},{3,2},{4,5},{5,4},{6,7},{7,6},{8,9},{9,8},{10,11... | collective-permute-start | bytes 49160 | tf_op jit(solution)/shard_map/ppermute | solution.py:330
  0.5 5.6 %collective-permute-start.1 = (bf16[2,8,4,128]{3,2,1,0:T(4,128)(2,1)}, bf16[2,8,4,128]{3,2,1,0:T(4,128)(2,1)S(1)}, u32[]{:S(2)}, u32[]{:S(2)}) collective-permute-start(bf16[2,8,4,128]{3,2,1,0:T(4,128)(2,1)} %coarse_ref.3), channel_id=1, source_target_pairs={{0,15},{1,2},{2,1},{3,4},{4,3},{5,6},{6,5},{7,8},{8,7},{9,10},{10,... | collective-permute-start | bytes 49160 | tf_op jit(solution)/shard_map/ppermute | solution.py:331
  6.2 0.0 collective-permute-start.2
  6.2 0.9 %copy.11.reg_in_ref = bf16[192,72]{1,0:T(8,128)(2,1)S(1)} copy(bf16[192,72]{0,1:T(8,128)(2,1)} %param.12) | data formatting | bytes 55296 | tf_op args[2]
  7.1 0.0 collective-permute-done.pair_ref
  7.1 0.8 %collective-permute-done.1.next_ref = bf16[2,8,4,128]{3,2,1,0:T(4,128)(2,1)S(1)} collective-permute-done((bf16[2,8,4,128]{3,2,1,0:T(4,128)(2,1)}, bf16[2,8,4,128]{3,2,1,0:T(4,128)(2,1)S(1)}, u32[]{:S(2)}, u32[]{:S(2)}) %collective-permute-start.1) | collective-permute-done | bytes 16416 | tf_op jit(solution)/shard_map/ppermute | solution.py:331
  7.8 5.0 %collective-permute-done.2.far_ref = bf16[2,8,4,128]{3,2,1,0:T(4,128)(2,1)S(1)} collective-permute-done((bf16[2,8,4,128]{3,2,1,0:T(4,128)(2,1)}, bf16[2,8,4,128]{3,2,1,0:T(4,128)(2,1)S(1)}, u32[]{:S(2)}, u32[]{:S(2)}) %collective-permute-start.2) | collective-permute-done | bytes 16416 | tf_op jit(solution)/shard_map/ppermute | solution.py:332
  12.8 1.3 %copy-done = bf16[2,192,1728]{2,1,0:T(8,128)(2,1)S(1)} copy-done((bf16[2,192,1728]{2,1,0:T(8,128)(2,1)S(1)}, bf16[2,192,1728]{2,1,0:T(8,128)(2,1)}, u32[]{:S(2)}) %copy-start) | copy-done | bytes 1327128
  14.2 0.7 %copy-done.2 = bf16[2,8,4,128]{3,2,1,0:T(4,128)(2,1)S(1)} copy-done((bf16[2,8,4,128]{3,2,1,0:T(4,128)(2,1)S(1)}, bf16[2,8,4,128]{3,2,1,0:T(4,128)(2,1)}, u32[]{:S(2)}) %copy-start.2) | copy-done | bytes 16408
  14.9 0.7 %copy-done.5 = bf16[4,192]{1,0:T(4,128)(2,1)S(1)} copy-done((bf16[4,192]{1,0:T(4,128)(2,1)S(1)}, bf16[4,192]{1,0:T(4,128)(2,1)}, u32[]{:S(2)}) %copy-start.5) | copy-done | bytes 1560
  15.6 5.5 %regress.1 = (bf16[192,512]{1,0:T(8,128)(2,1)S(1)}, f32[4,1024]{1,0:T(4,128)S(1)}, bf16[192,256]{1,0:T(8,128)(2,1)S(1)}, f32[4,512]{1,0:T(4,128)S(1)}, bf16[192,...) custom-call(bf16[2,8,4,128]{3,2,1,0:T(4,128)(2,1)S(1)} %copy-done.2, bf16[2,8,4,128]{3,2,1,0:T(4,128)(2,1)S(1)} %collective-permute-done.pair_ref, ...), custom_call_target="tpu_custom_call" | custom-call | tf_op jit(solution)/shard_map/regress/pallas_call | solution.py:333
  21.1 0.0 collective-permute-start.3
  21.1 0.5 %collective-permute-start.4 = (f32[4,512]{1,0:T(4,128)S(1)}, f32[4,512]{1,0:T(4,128)S(1)}, u32[]{:S(2)}, u32[]{:S(2)}) collective-permute-start(f32[4,512]{1,0:T(4,128)S(1)} %get-tuple-element.20), channel_id=1, source_target_pairs={{0,1},{1,0},{2,3},{3,2},{4,5},{5,4},{6,7},{7,6},{8,9},{9,8},{10,11... | collective-permute-start | bytes 24584 | tf_op jit(solution)/shard_map/ppermute | solution.py:353
  21.6 0.1 copy.12.diff_in_ref
  21.7 0.1 copy.13.diff_skip_ref
  21.9 0.6 %collective-permute-done.4.pair_reg_ref = f32[4,512]{1,0:T(4,128)S(1)} collective-permute-done((f32[4,512]{1,0:T(4,128)S(1)}, f32[4,512]{1,0:T(4,128)S(1)}, u32[]{:S(2)}, u32[]{:S(2)}) %collective-permute-start.4) | collective-permute-done | bytes 8224 | tf_op jit(solution)/shard_map/ppermute | solution.py:353
  22.5 0.0 collective-permute-done.3.pair_skip_ref
  22.5 5.6 %denoise.1 = (f32[4,512]{1,0:T(4,128)S(1)}, f32[4,512]{1,0:T(4,128)S(1)}, f32[4,256]{1,0:T(4,128)S(1)}, f32[4,256]{1,0:T(4,128)S(1)}) custom-call(bf16[2,8,4,128]{3,2,1,0:T(4,128)(2,1)S(1)} %copy-done.3, bf16[2,8,4,128]{3,2,1,0:T(4,128)(2,1)S(1)} %collective-permute-done.pair_ref, bf16[2,8,4,128]{3,2,1,0:T(4,128)(2,1)S(1)} %collective-permute-done.1.next_ref, ...), custom_call_target="tpu_custom_call" | custom-call | tf_op jit(solution)/shard_map/denoise/pallas_call | solution.py:354
  28.1 0.4 %collective-permute-start.5 = (f32[4,256]{1,0:T(4,128)S(1)}, f32[4,256]{1,0:T(4,128)S(1)}, u32[]{:S(2)}, u32[]{:S(2)}) collective-permute-start(f32[4,256]{1,0:T(4,128)S(1)} %get-tuple-element.25), channel_id=1, source_target_pairs={{0,1},{1,0},{2,3},{3,2},{4,5},{5,4},{6,7},{7,6},{8,9},{9,8},{10,11... | collective-permute-start | bytes 12296 | tf_op jit(solution)/shard_map/ppermute | solution.py:374
  28.5 0.8 %collective-permute-done.5.pair_ref = f32[4,256]{1,0:T(4,128)S(1)} collective-permute-done((f32[4,256]{1,0:T(4,128)S(1)}, f32[4,256]{1,0:T(4,128)S(1)}, u32[]{:S(2)}, u32[]{:S(2)}) %collective-permute-start.5) | collective-permute-done | bytes 4128 | tf_op jit(solution)/shard_map/ppermute | solution.py:374
  29.3 4.9 %collective-permute-done.6.next_ref = f32[4,256]{1,0:T(4,128)S(1)} collective-permute-done((f32[4,256]{1,0:T(4,128)S(1)}, f32[4,256]{1,0:T(4,128)S(1)}, u32[]{:S(2)}, u32[]{:S(2)}) %collective-permute-start.6) | collective-permute-done | bytes 4128 | tf_op jit(solution)/shard_map/ppermute | solution.py:375
  34.2 1.6 %collective-permute-start.7 = (f32[4,4,128]{2,1,0:T(4,128)S(1)}, f32[4,4,128]{2,1,0:T(4,128)S(1)}, u32[]{:S(2)}, u32[]{:S(2)}) collective-permute-start(f32[4,4,128]{2,1,0:T(4,128)S(1)} %get-tuple-element.28), channel_id=1, source_target_pairs={{0,16},{16,0},{1,17},{17,1},{2,18},{18,2},{3,19},{19,3},{4,20},{20... | collective-permute-start | bytes 24584 | tf_op jit(solution)/shard_map/ppermute | solution.py:378
  35.8 2.1 %collective-permute-done.7.got_ref = f32[4,4,128]{2,1,0:T(4,128)S(1)} collective-permute-done((f32[4,4,128]{2,1,0:T(4,128)S(1)}, f32[4,4,128]{2,1,0:T(4,128)S(1)}, u32[]{:S(2)}, u32[]{:S(2)}) %collective-permute-start.7) | collective-permute-done | bytes 8224 | tf_op jit(solution)/shard_map/ppermute | solution.py:378
  37.9 0.6 %output.1 = f32[1,2,4,4,128]{4,3,2,1,0:T(4,128)} custom-call(f32[4,4,128]{2,1,0:T(4,128)S(1)} %get-tuple-element.27.own_ref, f32[4,4,128]{2,1,0:T(4,128)S(1)} %collective-permute-done.7.got_ref), custom_call_target="tpu_custom_call" | custom-call | tf_op jit(solution)/shard_map/output/pallas_call | solution.py:379
  (19 shorter events, 0.1 us)
Async XLA Ops:
  0.0 22.5 %copy-start.3 = (bf16[2,8,4,128]{3,2,1,0:T(4,128)(2,1)S(1)}, bf16[2,8,4,128]{3,2,1,0:T(4,128)(2,1)}, u32[]{:S(2)}) copy-start(bf16[2,8,4,128]{3,2,1,0:T(4,128)(2,1)} %coarse_ref.3) | copy-start | bytes 49156
  0.0 22.5 %copy-start.7 = (f32[256]{0:T(256)S(1)}, f32[256]{0:T(256)}, u32[]{:S(2)}) copy-start(f32[256]{0:T(256)} %param.19) | copy-start | bytes 3076
  0.0 22.5 %copy-start.4 = (f32[2,4,8,128]{3,2,1,0:T(8,128)S(1)}, f32[2,4,8,128]{3,2,1,0:T(8,128)}, u32[]{:S(2)}) copy-start(f32[2,4,8,128]{3,2,1,0:T(8,128)} %noise_ref.1) | copy-start | bytes 98308
  0.0 22.5 %copy-start.6 = (bf16[4,256]{1,0:T(4,128)(2,1)S(1)}, bf16[4,256]{1,0:T(4,128)(2,1)}, u32[]{:S(2)}) copy-start(bf16[4,256]{1,0:T(4,128)(2,1)} %diff_out_ref.1) | copy-start | bytes 6148
  0.0 7.0 %collective-permute-start = (bf16[2,8,4,128]{3,2,1,0:T(4,128)(2,1)}, bf16[2,8,4,128]{3,2,1,0:T(4,128)(2,1)S(1)}, u32[]{:S(2)}, u32[]{:S(2)}) collective-permute-start(bf16[2,8,4,128]{3,2,1,0:T(4,128)(2,1)} %coarse_ref.3), channel_id=1, source_target_pairs={{0,1},{1,0},{2,3},{3,2},{4,5},{5,4},{6,7},{7,6},{8,9},{9,8},{10,11... | collective-permute-start | bytes 49160 | tf_op jit(solution)/shard_map/ppermute | solution.py:330
  0.5 7.3 %collective-permute-start.1 = (bf16[2,8,4,128]{3,2,1,0:T(4,128)(2,1)}, bf16[2,8,4,128]{3,2,1,0:T(4,128)(2,1)S(1)}, u32[]{:S(2)}, u32[]{:S(2)}) collective-permute-start(bf16[2,8,4,128]{3,2,1,0:T(4,128)(2,1)} %coarse_ref.3), channel_id=1, source_target_pairs={{0,15},{1,2},{2,1},{3,4},{4,3},{5,6},{6,5},{7,8},{8,7},{9,10},{10,... | collective-permute-start | bytes 49160 | tf_op jit(solution)/shard_map/ppermute | solution.py:331
  6.2 6.6 %collective-permute-start.2 = (bf16[2,8,4,128]{3,2,1,0:T(4,128)(2,1)}, bf16[2,8,4,128]{3,2,1,0:T(4,128)(2,1)S(1)}, u32[]{:S(2)}, u32[]{:S(2)}) collective-permute-start(bf16[2,8,4,128]{3,2,1,0:T(4,128)(2,1)} %coarse_ref.3), channel_id=1, source_target_pairs={{0,2},{1,15},{2,4},{3,1},{4,6},{5,3},{6,8},{7,5},{8,10},{9,7},{10,... | collective-permute-start | bytes 49160 | tf_op jit(solution)/shard_map/ppermute | solution.py:332
  12.8 1.3 %copy-start = (bf16[2,192,1728]{2,1,0:T(8,128)(2,1)S(1)}, bf16[2,192,1728]{2,1,0:T(8,128)(2,1)}, u32[]{:S(2)}) copy-start(bf16[2,192,1728]{2,1,0:T(8,128)(2,1)} %reg_mid_ref.1) | copy-start | bytes 3981316
  14.2 0.7 %copy-start.2 = (bf16[2,8,4,128]{3,2,1,0:T(4,128)(2,1)S(1)}, bf16[2,8,4,128]{3,2,1,0:T(4,128)(2,1)}, u32[]{:S(2)}) copy-start(bf16[2,8,4,128]{3,2,1,0:T(4,128)(2,1)} %coarse_ref.3) | copy-start | bytes 49156
  14.9 0.7 %copy-start.5 = (bf16[4,192]{1,0:T(4,128)(2,1)S(1)}, bf16[4,192]{1,0:T(4,128)(2,1)}, u32[]{:S(2)}) copy-start(bf16[4,192]{1,0:T(4,128)(2,1)} %reg_out_ref.1) | copy-start | bytes 4612
  15.6 6.1 %copy-start.9 = (bf16[256,144]{0,1:T(8,128)(2,1)S(1)}, bf16[256,144]{0,1:T(8,128)(2,1)}, u32[]{:S(2)}) copy-start(bf16[256,144]{0,1:T(8,128)(2,1)} %param.15) | copy-start | bytes 221188
  15.6 6.2 %copy-start.8 = (bf16[256,192]{0,1:T(8,128)(2,1)S(1)}, bf16[256,192]{0,1:T(8,128)(2,1)}, u32[]{:S(2)}) copy-start(bf16[256,192]{0,1:T(8,128)(2,1)} %param.16) | copy-start | bytes 294916
  15.6 6.9 %copy-start.1 = (bf16[256,2304]{1,0:T(8,128)(2,1)S(1)}, bf16[256,2304]{1,0:T(8,128)(2,1)}, u32[]{:S(2)}) copy-start(bf16[256,2304]{1,0:T(8,128)(2,1)} %diff_mid_ref.1) | copy-start | bytes 3538948
  21.1 1.4 %collective-permute-start.3 = (bf16[192,256]{1,0:T(8,128)(2,1)S(1)}, bf16[192,256]{1,0:T(8,128)(2,1)S(1)}, u32[]{:S(2)}, u32[]{:S(2)}) collective-permute-start(bf16[192,256]{1,0:T(8,128)(2,1)S(1)} %get-tuple-element.19), channel_id=1, source_target_pairs={{0,1},{1,0},{2,3},{3,2},{4,5},{5,4},{6,7},{7,6},{8,9},{9,8},{10,11... | collective-permute-start | bytes 294920 | tf_op jit(solution)/shard_map/ppermute | solution.py:352
  21.1 1.3 %collective-permute-start.4 = (f32[4,512]{1,0:T(4,128)S(1)}, f32[4,512]{1,0:T(4,128)S(1)}, u32[]{:S(2)}, u32[]{:S(2)}) collective-permute-start(f32[4,512]{1,0:T(4,128)S(1)} %get-tuple-element.20), channel_id=1, source_target_pairs={{0,1},{1,0},{2,3},{3,2},{4,5},{5,4},{6,7},{7,6},{8,9},{9,8},{10,11... | collective-permute-start | bytes 24584 | tf_op jit(solution)/shard_map/ppermute | solution.py:353
  28.1 1.2 %collective-permute-start.5 = (f32[4,256]{1,0:T(4,128)S(1)}, f32[4,256]{1,0:T(4,128)S(1)}, u32[]{:S(2)}, u32[]{:S(2)}) collective-permute-start(f32[4,256]{1,0:T(4,128)S(1)} %get-tuple-element.25), channel_id=1, source_target_pairs={{0,1},{1,0},{2,3},{3,2},{4,5},{5,4},{6,7},{7,6},{8,9},{9,8},{10,11... | collective-permute-start | bytes 12296 | tf_op jit(solution)/shard_map/ppermute | solution.py:374
  28.5 5.7 %collective-permute-start.6 = (f32[4,256]{1,0:T(4,128)S(1)}, f32[4,256]{1,0:T(4,128)S(1)}, u32[]{:S(2)}, u32[]{:S(2)}) collective-permute-start(f32[4,256]{1,0:T(4,128)S(1)} %get-tuple-element.26), channel_id=1, source_target_pairs={{0,15},{1,2},{2,1},{3,4},{4,3},{5,6},{6,5},{7,8},{8,7},{9,10},{10,... | collective-permute-start | bytes 12296 | tf_op jit(solution)/shard_map/ppermute | solution.py:375
  34.2 3.7 %collective-permute-start.7 = (f32[4,4,128]{2,1,0:T(4,128)S(1)}, f32[4,4,128]{2,1,0:T(4,128)S(1)}, u32[]{:S(2)}, u32[]{:S(2)}) collective-permute-start(f32[4,4,128]{2,1,0:T(4,128)S(1)} %get-tuple-element.28), channel_id=1, source_target_pairs={{0,16},{16,0},{1,17},{17,1},{2,18},{18,2},{3,19},{19,3},{4,20},{20... | collective-permute-start | bytes 24584 | tf_op jit(solution)/shard_map/ppermute | solution.py:378
where the time goes:
time: 38.8 us; the launch traced here: 38.6 us
  waiting for transfers between devices  14.2 us (37%)
  Pallas kernels  11.8 us (30%)
  starting transfers between devices  8.67 us (22%)
  local copies, waits for them, and re-layouts  3.83 us (10%)
    ppermute x1, starting transfers between devices, shards(): next_coarse = lax.ppermute(coarse, 'tile', nexts)  5.64 us
    pallas_call x1, Pallas kernels, shards(): call(denoise_kernel, 'denoise', [((fields, BAND * LANES), F32), ((fields,...  5.6 us
    pallas_call x1, Pallas kernels, shards(): call(regress_kernel, 'regress', [((width_r, BAND * LANES), BF16), ((field...  5.54 us
    ppermute x1, waiting for transfers between devices, shards(): far_coarse = lax.ppermute(coarse, 'tile', fars)  4.99 us
    ppermute x1, waiting for transfers between devices, shards(): next_band = lax.ppermute(send_next, 'tile', nexts)  4.91 us
    unnamed x23, local copies, waits for them, and re-layouts  3.83 us
    ppermute x1, waiting for transfers between devices, shards(): got = lax.ppermute(send, 'segment', swap)  2.12 us
    ppermute x1, starting transfers between devices, shards(): got = lax.ppermute(send, 'segment', swap)  1.59 us
  transfers between devices with their start and end apart: 8, of which 6 were waited for; matrix products, arithmetic and copies ran while one was open for 3% of the time, Pallas kernels for 0%

commit v1 on v0

--- a/solution.py
+++ b/solution.py
@@ -123,8 +123,18 @@
     return lax.rem(tile, 2) == 0, tile == 0, tile == count - 1
 
 
+def prepare_kernel(coarse_ref, noise_ref, own_ref, initial_ref):
+    sample = lax.axis_index("segment")
+    block = coarse_ref[sample].astype(F32)
+    for r in range(BAND):
+        own_ref[:, lanes(r)] = block[:, r, :]
+    block = noise_ref[sample]
+    for r in range(ROWS):
+        initial_ref[:, lanes(r)] = sigma_high * block[:, r, :]
+
+
 def regress_kernel(
-    coarse_ref, pair_ref, next_ref, far_ref, reg_in_ref, reg_mid_ref, reg_out_ref,
+    own_ref, pair_ref, next_ref, far_ref, reg_in_ref, reg_mid_ref, reg_out_ref,
     skip_ref, reg_ref, send_skip_ref, send_reg_ref, outer_skip_ref, outer_reg_ref,
     taps_in, hidden_a, hidden_b, taps_a, taps_b,
 ):
@@ -135,7 +145,8 @@
         block = ref[sample].astype(F32)
         return [block[:, r, :] for r in range(BAND)]
 
-    own, pair, across, far = (rows_of(ref) for ref in (coarse_ref, pair_ref, next_ref, far_ref))
+    own = [own_ref[:, lanes(r)] for r in range(BAND)]
+    pair, across, far = (rows_of(ref) for ref in (pair_ref, next_ref, far_ref))
     window = [jnp.where(even, far[2 + i], pair[2 + i]) for i in range(2)]
     window += [jnp.where(even, across[i], own[i]) for i in range(4)]
     window += [jnp.where(even, own[i], across[i]) for i in range(4)]
@@ -185,7 +196,7 @@
 
 
 def denoise_kernel(
-    coarse_ref, pair_ref, next_ref, noise_ref, skip_ref, reg_ref, pair_skip_ref, pair_reg_ref,
+    own_ref, pair_ref, next_ref, initial_ref, skip_ref, reg_ref, pair_skip_ref, pair_reg_ref,
     outer_skip_ref, outer_reg_ref, diff_in_ref, diff_skip_ref, diff_mid_ref, diff_out_ref, embed_ref,
     mean_ref, band_ref, send_pair_ref, send_next_ref,
     taps_in, skips, base, hidden, taps,
@@ -198,7 +209,8 @@
         block = ref[sample].astype(F32)
         return [block[:, r, :] for r in range(block.shape[1])]
 
-    own, pair, across = (rows_of(ref) for ref in (coarse_ref, pair_ref, next_ref))
+    own = [own_ref[:, lanes(r)] for r in range(BAND)]
+    pair, across = (rows_of(ref) for ref in (pair_ref, next_ref))
     coarse = [jnp.where(even, across[2 + i], pair[2 + i]) for i in range(2)]
     coarse += own
     coarse += [jnp.where(even, pair[i], across[i]) for i in range(2)]
@@ -231,8 +243,7 @@
 
     channels = diff_mid_ref.shape[0]
     embed = jnp.broadcast_to(embed_ref[...], (LANES, channels)).T
-    noise = rows_of(noise_ref)
-    initial = [sigma_high * n for n in noise]
+    initial = [initial_ref[:, lanes(r)] for r in range(ROWS)]
     step = 2
 
     def denoise(current, sigma_now):
@@ -306,76 +317,99 @@
     out_ref[0, 1] = jnp.where(lower, got, own)
 
 
-def call(kernel, name, outs, scratch=()):
+def call(kernel, name, outs, scratch=(), flops=0):
     return pl.pallas_call(
         kernel,
         name=name,
         out_shape=[jax.ShapeDtypeStruct(shape, dtype) for shape, dtype in outs],
-        scratch_shapes=[pltpu.VMEM(shape, dtype) for shape, dtype in scratch],
-        compiler_params=pltpu.CompilerParams(vmem_limit_bytes=32 * 1024 * 1024),
+        scratch_shapes=scratch,
+        compiler_params=pltpu.CompilerParams(vmem_limit_bytes=24 * 1024 * 1024),
+        cost_estimate=pl.CostEstimate(flops=flops, bytes_accessed=0, transcendentals=0),
     )
 
 
 def shards(
     coarse, noise_draw, reg_in, reg_mid, reg_out, diff_in, diff_skip, diff_mid, diff_out, noise_embed
 ):
-    tiles = lax.axis_size("tile")
-    pairs = [(i, i ^ 1) for i in range(tiles)]
-    nexts = [(i, (i - 1 if i % 2 == 0 else i + 1) % tiles) for i in range(tiles)]
-    fars = [(i, (i + 2 if i % 2 == 0 else i - 2) % tiles) for i in range(tiles)]
-    swap = [(0, 1), (1, 0)]
-    width_r, width_d, fields = reg_in.shape[0], diff_in.shape[0], reg_out.shape[0]
-    cells = ROWS * LANES
-
-    pair_coarse = lax.ppermute(coarse, "tile", pairs)
-    next_coarse = lax.ppermute(coarse, "tile", nexts)
-    far_coarse = lax.ppermute(coarse, "tile", fars)
+    tiles, segments = lax.axis_size("tile"), lax.axis_size("segment")
+    grid = [(s, t) for s in range(segments) for t in range(tiles)]
+
+    def permute(value, target):
+        edges = [(s * tiles + t, target(s, t)[0] * tiles + target(s, t)[1]) for s, t in grid]
+        return lax.ppermute(value, ("segment", "tile"), edges)
+
+    def pair(s, t):
+        return s, t ^ 1
+
+    def across(s, t):
+        to = t - 1 if t % 2 == 0 else t + 1
+        return (s, to) if 0 <= to < tiles else ((s + 1) % segments, t)
+
+    def far(s, t):
+        to = t + 2 if t % 2 == 0 else t - 2
+        return s, min(max(to, 0), tiles - 1)
+
+    def other(s, t):
+        return (s + 1) % segments, t
+
+    width_r, width_d, fields, inputs = reg_in.shape[0], diff_in.shape[0], reg_out.shape[0], coarse.shape[1]
+    cells, band_cells, edge_cells = ROWS * LANES, BAND * LANES, MARGIN * LANES
+    taps_cells = cells + 2 * LANES
+
+    pair_coarse = permute(coarse, pair)
+    next_coarse = permute(coarse, across)
+    far_coarse = permute(coarse, far)
+    own_coarse, initial = call(
+        prepare_kernel, "prepare", [((inputs, band_cells), F32), ((fields, cells), F32)], flops=4 * 10**9
+    )(coarse, noise_draw)
     skip, reg, send_skip, send_reg, outer_skip, outer_reg = call(
         regress_kernel,
         "regress",
         [
-            ((width_r, BAND * LANES), BF16),
+            ((width_r, band_cells), BF16),
             ((fields, cells), F32),
-            ((width_r, MARGIN * LANES), BF16),
-            ((fields, BAND * LANES), F32),
-            ((width_r, MARGIN * LANES), BF16),
-            ((fields, BAND * LANES), F32),
+            ((width_r, edge_cells), BF16),
+            ((fields, band_cells), F32),
+            ((width_r, edge_cells), BF16),
+            ((fields, band_cells), F32),
         ],
         [
-            ((reg_in.shape[1], cells), BF16),
-            ((width_r, cells), F32),
-            ((width_r, cells), F32),
-            ((3 * width_r, cells + 2 * LANES), BF16),
-            ((3 * width_r, cells + 2 * LANES), BF16),
+            pltpu.VMEM((reg_in.shape[1], cells), BF16),
+            pltpu.VMEM((width_r, cells), F32),
+            pltpu.VMEM((width_r, cells), F32),
+            pltpu.VMEM((3 * width_r, taps_cells), BF16),
+            pltpu.VMEM((3 * width_r, taps_cells), BF16),
         ],
-    )(coarse, pair_coarse, next_coarse, far_coarse, reg_in, reg_mid, reg_out)
-    pair_skip = lax.ppermute(send_skip, "tile", pairs)
-    pair_reg = lax.ppermute(send_reg, "tile", pairs)
+        flops=4 * 10**9,
+    )(own_coarse, pair_coarse, next_coarse, far_coarse, reg_in, reg_mid, reg_out)
+    pair_skip = permute(send_skip, pair)
+    pair_reg = permute(send_reg, pair)
     mean, band, send_pair, send_next = call(
         denoise_kernel,
         "denoise",
         [
-            ((fields, BAND * LANES), F32),
-            ((fields, BAND * LANES), F32),
-            ((fields, MARGIN * LANES), F32),
-            ((fields, MARGIN * LANES), F32),
+            ((fields, band_cells), F32),
+            ((fields, band_cells), F32),
+            ((fields, edge_cells), F32),
+            ((fields, edge_cells), F32),
         ],
         [
-            ((diff_in.shape[1], cells), BF16),
-            ((width_r, cells), BF16),
-            ((width_d, cells), F32),
-            ((width_d, cells), F32),
-            ((3 * width_d, cells + 2 * LANES), BF16),
+            pltpu.VMEM((diff_in.shape[1], cells), BF16),
+            pltpu.VMEM((width_r, cells), BF16),
+            pltpu.VMEM((width_d, cells), F32),
+            pltpu.VMEM((width_d, cells), F32),
+            pltpu.VMEM((3 * width_d, taps_cells), BF16),
         ],
+        flops=4 * 10**9,
     )(
-        coarse, pair_coarse, next_coarse, noise_draw, skip, reg, pair_skip, pair_reg,
+        own_coarse, pair_coarse, next_coarse, initial, skip, reg, pair_skip, pair_reg,
         outer_skip, outer_reg, diff_in, diff_skip, diff_mid, diff_out, noise_embed[None],
     )
-    pair_band = lax.ppermute(send_pair, "tile", pairs)
-    next_band = lax.ppermute(send_next, "tile", nexts)
+    pair_band = permute(send_pair, pair)
+    next_band = permute(send_next, across)
     piece = ((fields, BAND, LANES), F32)
     own, send = call(average_kernel, "average", [piece, piece])(mean, band, pair_band, next_band)
-    got = lax.ppermute(send, "segment", swap)
+    got = permute(send, other)
     (out,) = call(output_kernel, "output", [((1, 2, fields, BAND, LANES), F32)])(own, got)
     return out
 

time: 38.8 us -> 27.9 us (0.72)
  the two profiles are of different devices: /device:TPU:0 before, /device:TPU:24 now
where the time goes in v1:
time: 27.9 us; the launch traced here: 27.6 us
  Pallas kernels  11.8 us (42%)
  waiting for transfers between devices  8.25 us (30%)
  starting transfers between devices  4.88 us (17%)
  local copies, waits for them, and re-layouts  2.55 us (9%)
    ppermute x8, waiting for transfers between devices, permute(): return lax.ppermute(value, ('segment', 'tile'), edges)  8.25 us
    pallas_call x1, Pallas kernels, shards(): call(denoise_kernel, 'denoise', [((fields, band_cells), F32), ((fields, b...  5.61 us
    pallas_call x1, Pallas kernels, shards(): call(regress_kernel, 'regress', [((width_r, band_cells), BF16), ((fields,...  5.54 us
    ppermute x8, starting transfers between devices, permute(): return lax.ppermute(value, ('segment', 'tile'), edges)  4.88 us
    unnamed x23, local copies, waits for them, and re-layouts  2.55 us
    pallas_call x1, Pallas kernels, shards(): call(output_kernel, 'output', [((1, 2, fields, BAND, LANES), F32)])  0.61 us
  transfers between devices with their start and end apart: 8, of which 5 were waited for; matrix products, arithmetic and copies ran while one was open for 1% of the time, Pallas kernels for 0%

profile of v1, /device:TPU:24, one launch (start us, length us, event | category | flops | bytes accessed | tf_op | source)
XLA Modules:
  0.0 27.6 jit_solution(11420397986927785315)
XLA Ops:
  0.0 0.0 collective-permute-start
  0.0 1.5 %collective-permute-start.1 = (bf16[2,8,4,128]{3,2,1,0:T(4,128)(2,1)}, bf16[2,8,4,128]{3,2,1,0:T(4,128)(2,1)S(1)}, u32[]{:S(2)}, u32[]{:S(2)}) collective-permute-start(bf16[2,8,4,128]{3,2,1,0:T(4,128)(2,1)} %coarse_ref.1), channel_id=1, source_target_pairs={{0,16},{1,2},{2,1},{3,4},{4,3},{5,6},{6,5},{7,8},{8,7},{9,10},{10,... | collective-permute-start | bytes 49160 | tf_op jit(solution)/shard_map/ppermute | solution.py:339
  1.5 0.6 %collective-permute-start.2 = (bf16[2,8,4,128]{3,2,1,0:T(4,128)(2,1)}, bf16[2,8,4,128]{3,2,1,0:T(4,128)(2,1)S(1)}, u32[]{:S(2)}, u32[]{:S(2)}) collective-permute-start(bf16[2,8,4,128]{3,2,1,0:T(4,128)(2,1)} %coarse_ref.1), channel_id=1, source_target_pairs={{0,2},{1,0},{2,4},{3,1},{4,6},{5,3},{6,8},{7,5},{8,10},{9,7},{10,1... | collective-permute-start | bytes 49160 | tf_op jit(solution)/shard_map/ppermute | solution.py:339
  2.1 0.8 %copy-done.2 = f32[2,4,8,128]{3,2,1,0:T(8,128)S(1)} copy-done((f32[2,4,8,128]{3,2,1,0:T(8,128)S(1)}, f32[2,4,8,128]{3,2,1,0:T(8,128)}, u32[]{:S(2)}) %copy-start.2) | copy-done | bytes 32792
  2.9 0.7 %copy-done.3 = bf16[2,8,4,128]{3,2,1,0:T(4,128)(2,1)S(1)} copy-done((bf16[2,8,4,128]{3,2,1,0:T(4,128)(2,1)S(1)}, bf16[2,8,4,128]{3,2,1,0:T(4,128)(2,1)}, u32[]{:S(2)}) %copy-start.3) | copy-done | bytes 16408
  3.7 0.7 %copy-done.9 = bf16[192,72]{0,1:T(8,128)(2,1)S(1)} copy-done((bf16[192,72]{0,1:T(8,128)(2,1)S(1)}, bf16[192,72]{0,1:T(8,128)(2,1)}, u32[]{:S(2)}) %copy-start.9) | copy-done | bytes 27672
  4.4 0.1 copy.11.reg_in_ref
  4.5 1.8 %collective-permute-done.2.far_ref = bf16[2,8,4,128]{3,2,1,0:T(4,128)(2,1)S(1)} collective-permute-done((bf16[2,8,4,128]{3,2,1,0:T(4,128)(2,1)}, bf16[2,8,4,128]{3,2,1,0:T(4,128)(2,1)S(1)}, u32[]{:S(2)}, u32[]{:S(2)}) %collective-permute-start.2) | collective-permute-done | bytes 16416 | tf_op jit(solution)/shard_map/ppermute | solution.py:339
  6.4 0.0 copy-start.1
  6.4 0.0 copy-start.5
  6.4 0.0 copy-start.6
  6.4 5.5 %regress.1 = (bf16[192,512]{1,0:T(8,128)(2,1)S(1)}, f32[4,1024]{1,0:T(4,128)S(1)}, bf16[192,256]{1,0:T(8,128)(2,1)S(1)}, f32[4,512]{1,0:T(4,128)S(1)}, bf16[192,...) custom-call(f32[8,512]{1,0:T(8,128)S(1)} %get-tuple-element.19.own_ref, ...), custom_call_target="tpu_custom_call" | custom-call | flops 4000000000 | tf_op jit(solution)/shard_map/regress/pallas_call | solution.py:365
  11.9 0.5 %collective-permute-start.4 = (f32[4,512]{1,0:T(4,128)S(1)}, f32[4,512]{1,0:T(4,128)S(1)}, u32[]{:S(2)}, u32[]{:S(2)}) collective-permute-start(f32[4,512]{1,0:T(4,128)S(1)} %get-tuple-element.24), channel_id=1, source_target_pairs={{0,1},{1,0},{2,3},{3,2},{4,5},{5,4},{6,7},{7,6},{8,9},{9,8},{10,11... | collective-permute-start | bytes 24584 | tf_op jit(solution)/shard_map/ppermute | solution.py:339
  12.5 0.1 copy.12.diff_in_ref
  12.6 0.1 copy.13.diff_skip_ref
  12.7 0.6 %collective-permute-done.4.pair_reg_ref = f32[4,512]{1,0:T(4,128)S(1)} collective-permute-done((f32[4,512]{1,0:T(4,128)S(1)}, f32[4,512]{1,0:T(4,128)S(1)}, u32[]{:S(2)}, u32[]{:S(2)}) %collective-permute-start.4) | collective-permute-done | bytes 8224 | tf_op jit(solution)/shard_map/ppermute | solution.py:339
  13.3 5.6 %denoise.1 = (f32[4,512]{1,0:T(4,128)S(1)}, f32[4,512]{1,0:T(4,128)S(1)}, f32[4,256]{1,0:T(4,128)S(1)}, f32[4,256]{1,0:T(4,128)S(1)}) custom-call(f32[8,512]{1,0:T(8,128)S(1)} %get-tuple-element.19.own_ref, bf16[2,8,4,128]{3,2,1,0:T(4,128)(2,1)S(1)} %collective-permute-done.pair_ref, bf16[2,8,4,128]{3,2,1,0:T(4,128)(2,1)S(1)} %collective-permute-done.1.next_ref, ...), custom_call_target="tpu_custom_call" | custom-call | flops 4000000000 | tf_op jit(solution)/shard_map/denoise/pallas_call | solution.py:387
  18.9 0.4 %collective-permute-start.5 = (f32[4,256]{1,0:T(4,128)S(1)}, f32[4,256]{1,0:T(4,128)S(1)}, u32[]{:S(2)}, u32[]{:S(2)}) collective-permute-start(f32[4,256]{1,0:T(4,128)S(1)} %get-tuple-element.29), channel_id=1, source_target_pairs={{0,1},{1,0},{2,3},{3,2},{4,5},{5,4},{6,7},{7,6},{8,9},{9,8},{10,11... | collective-permute-start | bytes 12296 | tf_op jit(solution)/shard_map/ppermute | solution.py:339
  19.3 0.2 collective-permute-start.6
  19.5 0.6 %collective-permute-done.5.pair_ref = f32[4,256]{1,0:T(4,128)S(1)} collective-permute-done((f32[4,256]{1,0:T(4,128)S(1)}, f32[4,256]{1,0:T(4,128)S(1)}, u32[]{:S(2)}, u32[]{:S(2)}) %collective-permute-start.5) | collective-permute-done | bytes 4128 | tf_op jit(solution)/shard_map/ppermute | solution.py:339
  20.1 3.1 %collective-permute-done.6.next_ref = f32[4,256]{1,0:T(4,128)S(1)} collective-permute-done((f32[4,256]{1,0:T(4,128)S(1)}, f32[4,256]{1,0:T(4,128)S(1)}, u32[]{:S(2)}, u32[]{:S(2)}) %collective-permute-start.6) | collective-permute-done | bytes 4128 | tf_op jit(solution)/shard_map/ppermute | solution.py:339
  23.3 1.6 %collective-permute-start.7 = (f32[4,4,128]{2,1,0:T(4,128)S(1)}, f32[4,4,128]{2,1,0:T(4,128)S(1)}, u32[]{:S(2)}, u32[]{:S(2)}) collective-permute-start(f32[4,4,128]{2,1,0:T(4,128)S(1)} %get-tuple-element.32), channel_id=1, source_target_pairs={{0,16},{1,17},{2,18},{3,19},{4,20},{5,21},{6,22},{7,23},{8,24},{9,... | collective-permute-start | bytes 24584 | tf_op jit(solution)/shard_map/ppermute | solution.py:339
  24.8 2.1 %collective-permute-done.7.got_ref = f32[4,4,128]{2,1,0:T(4,128)S(1)} collective-permute-done((f32[4,4,128]{2,1,0:T(4,128)S(1)}, f32[4,4,128]{2,1,0:T(4,128)S(1)}, u32[]{:S(2)}, u32[]{:S(2)}) %collective-permute-start.7) | collective-permute-done | bytes 8224 | tf_op jit(solution)/shard_map/ppermute | solution.py:339
  27.0 0.6 %output.1 = f32[1,2,4,4,128]{4,3,2,1,0:T(4,128)} custom-call(f32[4,4,128]{2,1,0:T(4,128)S(1)} %get-tuple-element.31.own_ref, f32[4,4,128]{2,1,0:T(4,128)S(1)} %collective-permute-done.7.got_ref), custom_call_target="tpu_custom_call" | custom-call | tf_op jit(solution)/shard_map/output/pallas_call | solution.py:413
  (20 shorter events, 0.1 us)
Async XLA Ops:
  0.0 6.3 %copy-start = (bf16[2,192,1728]{2,1,0:T(8,128)(2,1)S(1)}, bf16[2,192,1728]{2,1,0:T(8,128)(2,1)}, u32[]{:S(2)}) copy-start(bf16[2,192,1728]{2,1,0:T(8,128)(2,1)} %reg_mid_ref.1) | copy-start | bytes 3981316
  0.0 4.5 %collective-permute-start = (bf16[2,8,4,128]{3,2,1,0:T(4,128)(2,1)}, bf16[2,8,4,128]{3,2,1,0:T(4,128)(2,1)S(1)}, u32[]{:S(2)}, u32[]{:S(2)}) collective-permute-start(bf16[2,8,4,128]{3,2,1,0:T(4,128)(2,1)} %coarse_ref.1), channel_id=1, source_target_pairs={{0,1},{1,0},{2,3},{3,2},{4,5},{5,4},{6,7},{7,6},{8,9},{9,8},{10,11... | collective-permute-start | bytes 49160 | tf_op jit(solution)/shard_map/ppermute | solution.py:339
  0.0 4.5 %collective-permute-start.1 = (bf16[2,8,4,128]{3,2,1,0:T(4,128)(2,1)}, bf16[2,8,4,128]{3,2,1,0:T(4,128)(2,1)S(1)}, u32[]{:S(2)}, u32[]{:S(2)}) collective-permute-start(bf16[2,8,4,128]{3,2,1,0:T(4,128)(2,1)} %coarse_ref.1), channel_id=1, source_target_pairs={{0,16},{1,2},{2,1},{3,4},{4,3},{5,6},{6,5},{7,8},{8,7},{9,10},{10,... | collective-permute-start | bytes 49160 | tf_op jit(solution)/shard_map/ppermute | solution.py:339
  1.5 4.8 %collective-permute-start.2 = (bf16[2,8,4,128]{3,2,1,0:T(4,128)(2,1)}, bf16[2,8,4,128]{3,2,1,0:T(4,128)(2,1)S(1)}, u32[]{:S(2)}, u32[]{:S(2)}) collective-permute-start(bf16[2,8,4,128]{3,2,1,0:T(4,128)(2,1)} %coarse_ref.1), channel_id=1, source_target_pairs={{0,2},{1,0},{2,4},{3,1},{4,6},{5,3},{6,8},{7,5},{8,10},{9,7},{10,1... | collective-permute-start | bytes 49160 | tf_op jit(solution)/shard_map/ppermute | solution.py:339
  2.1 0.8 %copy-start.2 = (f32[2,4,8,128]{3,2,1,0:T(8,128)S(1)}, f32[2,4,8,128]{3,2,1,0:T(8,128)}, u32[]{:S(2)}) copy-start(f32[2,4,8,128]{3,2,1,0:T(8,128)} %noise_ref.1) | copy-start | bytes 98308
  2.9 0.7 %copy-start.3 = (bf16[2,8,4,128]{3,2,1,0:T(4,128)(2,1)S(1)}, bf16[2,8,4,128]{3,2,1,0:T(4,128)(2,1)}, u32[]{:S(2)}) copy-start(bf16[2,8,4,128]{3,2,1,0:T(4,128)(2,1)} %coarse_ref.1) | copy-start | bytes 49156
  3.6 0.8 %copy-start.9 = (bf16[192,72]{0,1:T(8,128)(2,1)S(1)}, bf16[192,72]{0,1:T(8,128)(2,1)}, u32[]{:S(2)}) copy-start(bf16[192,72]{0,1:T(8,128)(2,1)} %param.12) | copy-start | bytes 82948
  3.6 2.7 %copy-start.4 = (bf16[4,192]{1,0:T(4,128)(2,1)S(1)}, bf16[4,192]{1,0:T(4,128)(2,1)}, u32[]{:S(2)}) copy-start(bf16[4,192]{1,0:T(4,128)(2,1)} %reg_out_ref.1) | copy-start | bytes 4612
  6.3 6.1 %copy-start.8 = (bf16[256,144]{0,1:T(8,128)(2,1)S(1)}, bf16[256,144]{0,1:T(8,128)(2,1)}, u32[]{:S(2)}) copy-start(bf16[256,144]{0,1:T(8,128)(2,1)} %param.15) | copy-start | bytes 221188
  6.4 6.2 %copy-start.7 = (bf16[256,192]{0,1:T(8,128)(2,1)S(1)}, bf16[256,192]{0,1:T(8,128)(2,1)}, u32[]{:S(2)}) copy-start(bf16[256,192]{0,1:T(8,128)(2,1)} %param.16) | copy-start | bytes 294916
  6.4 6.9 %copy-start.1 = (bf16[256,2304]{1,0:T(8,128)(2,1)S(1)}, bf16[256,2304]{1,0:T(8,128)(2,1)}, u32[]{:S(2)}) copy-start(bf16[256,2304]{1,0:T(8,128)(2,1)} %diff_mid_ref.1) | copy-start | bytes 3538948
  6.4 6.9 %copy-start.5 = (bf16[4,256]{1,0:T(4,128)(2,1)S(1)}, bf16[4,256]{1,0:T(4,128)(2,1)}, u32[]{:S(2)}) copy-start(bf16[4,256]{1,0:T(4,128)(2,1)} %diff_out_ref.1) | copy-start | bytes 6148
  6.4 6.9 %copy-start.6 = (f32[256]{0:T(256)S(1)}, f32[256]{0:T(256)}, u32[]{:S(2)}) copy-start(f32[256]{0:T(256)} %param.19) | copy-start | bytes 3076
  11.9 1.4 %collective-permute-start.3 = (bf16[192,256]{1,0:T(8,128)(2,1)S(1)}, bf16[192,256]{1,0:T(8,128)(2,1)S(1)}, u32[]{:S(2)}, u32[]{:S(2)}) collective-permute-start(bf16[192,256]{1,0:T(8,128)(2,1)S(1)} %get-tuple-element.23), channel_id=1, source_target_pairs={{0,1},{1,0},{2,3},{3,2},{4,5},{5,4},{6,7},{7,6},{8,9},{9,8},{10,11... | collective-permute-start | bytes 294920 | tf_op jit(solution)/shard_map/ppermute | solution.py:339
  11.9 1.3 %collective-permute-start.4 = (f32[4,512]{1,0:T(4,128)S(1)}, f32[4,512]{1,0:T(4,128)S(1)}, u32[]{:S(2)}, u32[]{:S(2)}) collective-permute-start(f32[4,512]{1,0:T(4,128)S(1)} %get-tuple-element.24), channel_id=1, source_target_pairs={{0,1},{1,0},{2,3},{3,2},{4,5},{5,4},{6,7},{7,6},{8,9},{9,8},{10,11... | collective-permute-start | bytes 24584 | tf_op jit(solution)/shard_map/ppermute | solution.py:339
  18.9 1.2 %collective-permute-start.5 = (f32[4,256]{1,0:T(4,128)S(1)}, f32[4,256]{1,0:T(4,128)S(1)}, u32[]{:S(2)}, u32[]{:S(2)}) collective-permute-start(f32[4,256]{1,0:T(4,128)S(1)} %get-tuple-element.29), channel_id=1, source_target_pairs={{0,1},{1,0},{2,3},{3,2},{4,5},{5,4},{6,7},{7,6},{8,9},{9,8},{10,11... | collective-permute-start | bytes 12296 | tf_op jit(solution)/shard_map/ppermute | solution.py:339
  19.3 3.9 %collective-permute-start.6 = (f32[4,256]{1,0:T(4,128)S(1)}, f32[4,256]{1,0:T(4,128)S(1)}, u32[]{:S(2)}, u32[]{:S(2)}) collective-permute-start(f32[4,256]{1,0:T(4,128)S(1)} %get-tuple-element.30), channel_id=1, source_target_pairs={{0,16},{1,2},{2,1},{3,4},{4,3},{5,6},{6,5},{7,8},{8,7},{9,10},{10,... | collective-permute-start | bytes 12296 | tf_op jit(solution)/shard_map/ppermute | solution.py:339
  23.3 3.7 %collective-permute-start.7 = (f32[4,4,128]{2,1,0:T(4,128)S(1)}, f32[4,4,128]{2,1,0:T(4,128)S(1)}, u32[]{:S(2)}, u32[]{:S(2)}) collective-permute-start(f32[4,4,128]{2,1,0:T(4,128)S(1)} %get-tuple-element.32), channel_id=1, source_target_pairs={{0,16},{1,17},{2,18},{3,19},{4,20},{5,21},{6,22},{7,23},{8,24},{9,... | collective-permute-start | bytes 24584 | tf_op jit(solution)/shard_map/ppermute | solution.py:339

commit v2 on v1

v2 whole, which is shorter than its diff:
```python
import math

import jax
import jax.numpy as jnp
from jax import lax
from jax.experimental import pallas as pl
from jax.experimental.pallas import tpu as pltpu
from jax.sharding import PartitionSpec as P

GROUPS = 32
LANES = 128
BAND = 4
MARGIN = 2
ROWS = BAND + 2 * MARGIN
STEP = 2
TILE = 256

sigma_high = 4.0
sigma_low = 0.5
sigma_data = 0.5

F32 = jnp.float32
BF16 = jnp.bfloat16


def lanes(first, count=1):
    return slice(first * LANES, (first + count) * LANES)


def col_shifts(chunk):
    index = jnp.int16 if chunk.dtype == BF16 else jnp.int32
    lane = lax.broadcasted_iota(index, chunk.shape, 1)
    zero = jnp.zeros_like(chunk)
    before = jnp.where(lane == 0, zero, pltpu.roll(chunk, 1, 1))
    after = jnp.where(lane == LANES - 1, zero, pltpu.roll(chunk, LANES - 1, 1))
    return before, chunk, after


def group_total(part):
    channels = part.shape[0]
    size = channels // GROUPS
    if size == 8:
        total = jnp.sum(part.reshape(GROUPS, 8, LANES), axis=(1, 2), keepdims=True)
        return jnp.broadcast_to(total, (GROUPS, 8, LANES)).reshape(channels, LANES)
    blocks = channels // 24
    tiles = part.reshape(blocks, 3, 8, LANES)
    row = lax.broadcasted_iota(jnp.int32, (blocks, 8, LANES), 1)
    v0, v1, v2 = tiles[:, 0], tiles[:, 1], tiles[:, 2]
    zero = jnp.zeros_like(v0)
    sums = (
        jnp.where(row < 6, v0, zero),
        jnp.where(row >= 6, v0, zero) + jnp.where(row < 4, v1, zero),
        jnp.where(row >= 4, v1, zero) + jnp.where(row < 2, v2, zero),
        jnp.where(row >= 2, v2, zero),
    )
    t0, t1, t2, t3 = (
        jnp.broadcast_to(jnp.sum(s, axis=(1, 2), keepdims=True), (blocks, 8, LANES)) for s in sums
    )
    m0 = jnp.where(row < 6, t0, t1)
    m1 = jnp.where(row < 4, t1, t2)
    m2 = jnp.where(row < 2, t2, t3)
    return jnp.stack([m0, m1, m2], axis=1).reshape(channels, LANES)


class Norm:
    def __init__(self, channels):
        self.size = channels // GROUPS * LANES
        self.shift = None

    def add(self, chunk):
        rows = [chunk[:, lanes(r)] for r in range(STEP)]
        if self.shift is None:
            self.shift = group_total(sum(rows[1:], rows[0])) * (1.0 / (STEP * self.size))
            self.first = self.second = jnp.zeros_like(self.shift)
        for row in rows:
            away = row - self.shift
            self.first = self.first + away
            self.second = self.second + away * away

    def scales(self):
        share = 1.0 / (ROWS * self.size)
        mean = group_total(self.first) * share
        square = group_total(self.second) * share
        return self.shift + mean, 0.5 * lax.rsqrt(square - mean * mean + 1e-5)


def silu(rows, scales):
    centre, half = scales
    v = (rows - centre) * half
    return (v + v * jnp.tanh(v)).astype(BF16)


def depths(channels):
    whole = 3 * channels // TILE * TILE
    return whole, 3 * channels - whole


def packed(weight):
    whole, rest = depths(weight.shape[0])
    starts = [a * (whole + rest) for a in range(3)]
    parts = [weight[:, at : at + whole] for at in starts]
    if rest:
        parts += [weight[:, at + whole : at + whole + rest] for at in starts]
    return jnp.concatenate(parts, axis=1)


def patch_shapes(channels):
    whole, rest = depths(channels)
    hidden = [((channels, STEP * LANES), F32)] * (ROWS // STEP)
    taps = [((whole, LANES), BF16)] * ROWS
    return hidden, taps, [((3 * rest, LANES), BF16)] * ROWS if rest else []


class Patch:
    def __init__(self, hidden, hidden_next, taps, left):
        self.hidden, self.hidden_next, self.taps, self.left = hidden, hidden_next, taps, left
        self.channels = hidden[0].shape[0]
        self.whole, self.rest = depths(self.channels)

    def start(self, first_rows):
        norm = Norm(self.channels)
        for k, ref in enumerate(self.hidden):
            chunk = first_rows(k * STEP)
            ref[...] = chunk
            norm.add(chunk)
        self.scales = norm.scales()
        if self.rest:
            blank = jnp.zeros((self.rest, LANES), BF16)
            self.left[0][: self.rest, :] = blank
            self.left[-1][2 * self.rest :, :] = blank

    def rows(self, row):
        return self.hidden[row // STEP][:, lanes(row % STEP)]

    def store(self, row):
        shifts = jnp.concatenate(col_shifts(silu(self.rows(row), self.scales)), axis=0)
        self.taps[row][...] = shifts[: self.whole]
        if self.rest:
            for a in range(3):
                if 0 <= row + 1 - a < ROWS:
                    self.left[row + 1 - a][a * self.rest : (a + 1) * self.rest, :] = shifts[self.whole :]

    def act_steps(self):
        return [lambda r=r: self.store(r) for r in range(ROWS)]

    def conv_steps(self, weight):
        norm = Norm(self.channels)
        source, target = self.hidden, self.hidden_next

        def tap_row(r):
            return self.taps[r][...] if 0 <= r < ROWS else jnp.zeros((self.whole, LANES), BF16)

        def step(k):
            first = k * STEP
            taps = [
                jnp.concatenate([tap_row(first + i + a - 1) for i in range(STEP)], axis=1) for a in range(3)
            ]
            if self.rest:
                taps.append(jnp.concatenate([self.left[first + i][...] for i in range(STEP)], axis=1))
            chunk = source[k][...] + jnp.dot(
                weight(), jnp.concatenate(taps, axis=0), preferred_element_type=F32
            )
            target[k][...] = chunk
            norm.add(chunk)
            if k == len(source) - 1:
                self.scales = norm.scales()
                self.hidden, self.hidden_next = target, source

        return [lambda k=k: step(k) for k in range(len(source))]


def run(*columns):
    longest = max(len(c) for c in columns)
    done = [0] * len(columns)
    for i in range(1, longest + 1):
        for k, column in enumerate(columns):
            while done[k] * longest < i * len(column):
                column[done[k]]()
                done[k] += 1


def input_taps(rows, out_ref):
    if rows[0].shape[0] % 16 == 0:
        rows = [row.astype(BF16) for row in rows]
    shifted = [col_shifts(row) for row in rows]
    blank = jnp.zeros_like(rows[0])
    for i in range(ROWS):
        pieces = []
        for a in range(3):
            pieces.extend(shifted[i + a - 1] if 0 <= i + a - 1 < ROWS else [blank] * 3)
        out_ref[:, lanes(i)] = jnp.concatenate(pieces, axis=0).astype(BF16)


def place():
    tile = lax.axis_index("tile")
    count = lax.axis_size("tile")
    return lax.rem(tile, 2) == 0, tile == 0, tile == count - 1


def prepare_kernel(embed_ref, embed_out):
    embed_out[...] = jnp.broadcast_to(embed_ref[...], embed_out.shape[::-1]).T


def weights_kernel(
    embed_ref, reg_in_ref, reg_mid_ref, diff_in_ref, diff_skip_ref,
    reg_in_out, reg_mid_out, diff_in_out, diff_skip_out,
):
    for source, target in (
        (reg_in_ref, reg_in_out), (diff_in_ref, diff_in_out), (diff_skip_ref, diff_skip_out)
    ):
        target[...] = source[...].astype(F32).T.astype(BF16)
    for block in range(reg_mid_ref.shape[0]):
        reg_mid_out[block] = packed(reg_mid_ref[block])


def coarse_window(coarse_ref, pair_ref, next_ref, far_ref):
    even, first, last = place()
    sample = lax.axis_index("segment")
    own, pair, across, far = (
        [ref[sample].astype(F32)[:, r, :] for r in range(BAND)]
        for ref in (coarse_ref, pair_ref, next_ref, far_ref)
    )
    alone = jnp.logical_or(jnp.logical_and(even, first), jnp.logical_and(jnp.logical_not(even), last))
    across, far = ([jnp.where(alone, jnp.zeros_like(r), r) for r in rows] for rows in (across, far))
    low = far[2:] + across + own + pair[:2]
    high = pair[2:] + own + across + far[:2]
    return even, [jnp.where(even, a, b) for a, b in zip(low, high)]


def own_rows(even, window):
    return [jnp.where(even, window[i + BAND], window[i]) for i in range(ROWS)]


def regress_kernel(
    coarse_ref, pair_ref, next_ref, far_ref, reg_in_ref, reg_mid_ref, reg_out_ref,
    rows_ref, skip_ref, reg_ref, send_skip_ref, send_reg_ref, *refs,
):
    taps_in_a, taps_in_b = refs[-2:]
    even, window = coarse_window(coarse_ref, pair_ref, next_ref, far_ref)
    rows_a = own_rows(even, window)
    rows_b = [jnp.where(even, window[i], window[i + BAND]) for i in range(ROWS)]
    for r in range(ROWS):
        rows_ref[:, lanes(r)] = rows_a[r]
    half = ROWS // STEP
    hidden_out, taps_out, left_out = refs[:half], refs[half : half + ROWS], refs[half + ROWS : half + 2 * ROWS]
    refs = refs[half + 2 * ROWS : -2]
    spare, refs = refs[:half], refs[half:]
    blocks = reg_mid_ref.shape[0]
    hidden_b = (spare, hidden_out) if blocks % 2 == 0 else (hidden_out, spare)
    outer = Patch(*hidden_b, taps_out, left_out)
    own = Patch(refs[:half], refs[half : 2 * half], refs[2 * half : 2 * half + ROWS], refs[2 * half + ROWS :])
    reg_in = reg_in_ref[...]
    for patch, rows, taps_in in ((own, rows_a, taps_in_a), (outer, rows_b, taps_in_b)):
        input_taps(rows, taps_in)
        patch.start(
            lambda r: jnp.dot(reg_in, taps_in[:, lanes(r, STEP)], preferred_element_type=F32)
        )

    for block in range(blocks):
        def weight():
            return reg_mid_ref[block]

        if block == 0:
            run(own.act_steps())
        run(own.conv_steps(weight), outer.act_steps())
        if block < blocks - 1:
            run(outer.conv_steps(weight), own.act_steps())

    for i in range(BAND):
        skip_ref[:, lanes(i)] = own.rows(MARGIN + i).astype(BF16)
    for i in range(MARGIN):
        send_skip_ref[:, lanes(i)] = jnp.where(even, own.rows(4 + i), own.rows(2 + i)).astype(BF16)
    reg = []
    for hidden in own.hidden:
        act = silu(hidden[...], [jnp.concatenate([s] * STEP, axis=1) for s in own.scales])
        reg.append(jnp.dot(reg_out_ref[...], act, preferred_element_type=F32))
    for k, part in enumerate(reg):
        reg_ref[:, lanes(k * STEP, STEP)] = part
    for k in range(half // 2):
        send_reg_ref[:, lanes(k * STEP, STEP)] = jnp.where(even, reg[half // 2 + k], reg[k])


def outer_kernel(reg_mid_ref, reg_out_ref, *refs):
    even, first, last = place()
    half = ROWS // STEP
    outer_skip_ref, outer_reg_ref = refs[half + 2 * ROWS : half + 2 * ROWS + 2]
    outer = Patch(
        refs[:half], refs[half + 2 * ROWS + 2 :], refs[half : half + ROWS], refs[half + ROWS : half + 2 * ROWS]
    )
    block = reg_mid_ref.shape[0] - 1
    run(outer.conv_steps(lambda: reg_mid_ref[block]))
    for i in range(MARGIN):
        outer_skip_ref[:, lanes(i)] = jnp.where(even, outer.rows(4 + i), outer.rows(2 + i)).astype(BF16)
    scales = [jnp.concatenate([s] * STEP, axis=1) for s in outer.scales]
    for k in range(half // 2):
        rows = jnp.where(even, outer.hidden[half // 2 + k][...], outer.hidden[k][...])
        outer_reg_ref[:, lanes(k * STEP, STEP)] = jnp.dot(
            reg_out_ref[...], silu(rows, scales), preferred_element_type=F32
        )


def denoise_kernel(
    rows_ref, noise_ref, skip_ref, reg_ref, pair_skip_ref, pair_reg_ref,
    outer_skip_ref, outer_reg_ref, diff_in_ref, diff_skip_ref, diff_mid_ref, diff_out_ref, embed_ref,
    mean_ref, band_ref, send_pair_ref, send_next_ref,
    taps_in, skips, base, *refs,
):
    even, first, last = place()
    coarse = [rows_ref[:, lanes(r)] for r in range(ROWS)]
    reg = [reg_ref[:, lanes(r)] for r in range(ROWS)]
    up = [jnp.where(even, outer_reg_ref[:, lanes(i)], pair_reg_ref[:, lanes(i)]) for i in range(4)]
    down = [jnp.where(even, pair_reg_ref[:, lanes(i)], outer_reg_ref[:, lanes(i)]) for i in range(4)]
    mean = []
    for r in range(ROWS):
        both = 0.5 * (reg[r] + (up[r] if r < 4 else down[r - 4]))
        if r < MARGIN:
            mean.append(jnp.where(first, jnp.zeros_like(both), both))
        elif r < 4:
            mean.append(jnp.where(first, reg[r], both))
        elif r < MARGIN + BAND:
            mean.append(jnp.where(last, reg[r], both))
        else:
            mean.append(jnp.where(last, jnp.zeros_like(both), both))
    for i in range(BAND):
        mean_ref[:, lanes(i)] = mean[MARGIN + i]
    mean = [m.astype(BF16).astype(F32) for m in mean]
    for i in range(2):
        low = jnp.where(even, outer_skip_ref[:, lanes(i)], pair_skip_ref[:, lanes(i)])
        high = jnp.where(even, pair_skip_ref[:, lanes(i)], outer_skip_ref[:, lanes(i)])
        skips[:, lanes(i)] = jnp.where(first, jnp.zeros_like(low), low)
        skips[:, lanes(6 + i)] = jnp.where(last, jnp.zeros_like(high), high)
    skips[:, lanes(MARGIN, BAND)] = skip_ref[...]
    embed = embed_ref[...]
    noise = noise_ref[lax.axis_index("segment")]
    initial = [sigma_high * noise[:, r, :] for r in range(ROWS)]
    half = ROWS // STEP
    patch = Patch(refs[:half], refs[half : 2 * half], refs[2 * half : 2 * half + ROWS], refs[2 * half + ROWS :])

    def denoise(current, sigma_now):
        total_var = sigma_now * sigma_now + sigma_data * sigma_data
        input_scale = 1.0 / math.sqrt(total_var)
        skip_coef = sigma_data * sigma_data / total_var
        out_coef = sigma_now * sigma_data / math.sqrt(total_var)
        input_taps(
            [
                jnp.concatenate([input_scale * current[r], coarse[r], mean[r]], axis=0)
                for r in range(ROWS)
            ],
            taps_in,
        )
        shift = jnp.concatenate([(math.log(sigma_now) / 4.0) * embed] * STEP, axis=1)

        def first_rows(r):
            if sigma_now == sigma_high:
                base[:, lanes(r, STEP)] = jnp.dot(
                    diff_skip_ref[...], skips[:, lanes(r, STEP)], preferred_element_type=F32
                )
            fresh = jnp.dot(diff_in_ref[...], taps_in[:, lanes(r, STEP)], preferred_element_type=F32)
            return fresh + base[:, lanes(r, STEP)] + shift

        patch.start(first_rows)
        acts = patch.act_steps()
        convs = patch.conv_steps(lambda: diff_mid_ref[...])
        for step in acts[: STEP + 1]:
            step()
        acts = acts[STEP + 1 :]
        for step in convs:
            step()
            for _ in range(min(STEP, len(acts))):
                acts.pop(0)()
        result = []
        scales = [jnp.concatenate([s] * STEP, axis=1) for s in patch.scales]
        for k, ref in enumerate(patch.hidden):
            out = jnp.dot(diff_out_ref[...], silu(ref[...], scales), preferred_element_type=F32)
            for i in range(STEP):
                result.append(skip_coef * current[k * STEP + i] + out_coef * out[:, lanes(i)])
        return result

    denoised = denoise(initial, sigma_high)
    stepped = [
        x + (sigma_low - sigma_high) * (x - d) / sigma_high for x, d in zip(initial, denoised)
    ]
    final = denoise(stepped, sigma_low)
    for i in range(BAND):
        band_ref[:, lanes(i)] = final[MARGIN + i]
    for i in range(MARGIN):
        send_pair_ref[:, lanes(i)] = jnp.where(even, final[6 + i], final[i])
        send_next_ref[:, lanes(i)] = jnp.where(even, final[i], final[6 + i])


def average_kernel(mean_ref, band_ref, pair_ref, next_ref, own_ref, send_ref):
    even, first, last = place()
    lower = lax.axis_index("segment") == 0
    for i in range(BAND):
        here = band_ref[:, lanes(i)]
        mean = mean_ref[:, lanes(i)]
        j = i % MARGIN
        if i < MARGIN:
            other = jnp.where(even, next_ref[:, lanes(j)], pair_ref[:, lanes(j)])
            alone = first
        else:
            other = jnp.where(even, pair_ref[:, lanes(j)], next_ref[:, lanes(j)])
            alone = last
        value = jnp.where(alone, here, 0.5 * (here + other)) + mean.astype(BF16).astype(F32)
        own_ref[:, i, :] = jnp.where(lower, mean, value)
        send_ref[:, i, :] = jnp.where(lower, value, mean)


def output_kernel(own_ref, got_ref, out_ref):
    lower = lax.axis_index("segment") == 0
    own, got = own_ref[...], got_ref[...]
    out_ref[0, 0] = jnp.where(lower, own, got)
    out_ref[0, 1] = jnp.where(lower, got, own)


def scratch(buffers):
    return [pltpu.VMEM(shape, dtype) for shape, dtype in buffers]


def call(kernel, name, outs, scratch_shapes=(), flops=0):
    return pl.pallas_call(
        kernel,
        name=name,
        out_shape=[jax.ShapeDtypeStruct(shape, dtype) for shape, dtype in outs],
        scratch_shapes=scratch_shapes,
        compiler_params=pltpu.CompilerParams(vmem_limit_bytes=24 * 1024 * 1024),
        cost_estimate=pl.CostEstimate(flops=flops, bytes_accessed=0, transcendentals=0),
    )


def shards(
    coarse, noise_draw, reg_in, reg_mid, reg_out, diff_in, diff_skip, diff_mid, diff_out, noise_embed
):
    tiles, segments = lax.axis_size("tile"), lax.axis_size("segment")
    grid = [(s, t) for s in range(segments) for t in range(tiles)]

    def permute(value, target):
        edges = [(s * tiles + t, target(s, t)[0] * tiles + target(s, t)[1]) for s, t in grid]
        return lax.ppermute(value, ("segment", "tile"), edges)

    def pair(s, t):
        return s, t ^ 1

    def across(s, t):
        to = t - 1 if t % 2 == 0 else t + 1
        return (s, to) if 0 <= to < tiles else ((s + 1) % segments, t)

    def other(s, t):
        return (s + 1) % segments, t

    width_r, width_d, fields, inputs = reg_in.shape[0], diff_in.shape[0], reg_out.shape[0], coarse.shape[1]
    cells, band_cells, edge_cells = ROWS * LANES, BAND * LANES, MARGIN * LANES
    taps_cells = cells + 2 * LANES

    pair_coarse = permute(coarse, pair)
    next_coarse = permute(coarse, across)
    far_coarse = permute(pair_coarse, across)
    (embed,) = call(prepare_kernel, "prepare", [((width_d, LANES), F32)], flops=4 * 10**9)(noise_embed[None])
    reg_in, reg_mid, diff_in, diff_skip = call(
        weights_kernel,
        "weights",
        [(w.shape, BF16) for w in (reg_in, reg_mid, diff_in, diff_skip)],
        flops=4 * 10**9,
    )(embed, reg_in.T, reg_mid, diff_in.T, diff_skip.T)
    hidden_r, taps_r, left_r = patch_shapes(width_r)
    hidden_d, taps_d, left_d = patch_shapes(width_d)
    rows, skip, reg, send_skip, send_reg, *outer = call(
        regress_kernel,
        "regress",
        [
            ((inputs, cells), F32),
            ((width_r, band_cells), BF16),
            ((fields, cells), F32),
            ((width_r, edge_cells), BF16),
            ((fields, band_cells), F32),
        ]
        + hidden_r + taps_r + left_r,
        scratch(hidden_r * 3 + taps_r + left_r + [((reg_in.shape[1], cells), BF16)] * 2),
        flops=3 * 10**9,
    )(coarse, pair_coarse, next_coarse, far_coarse, reg_in, reg_mid, reg_out)
    pair_skip = permute(send_skip, pair)
    pair_reg = permute(send_reg, pair)
    outer_skip, outer_reg = call(
        outer_kernel,
        "outer",
        [((width_r, edge_cells), BF16), ((fields, band_cells), F32)],
        scratch(hidden_r),
        flops=10**9,
    )(reg_mid, reg_out, *outer)
    mean, band, send_pair, send_next = call(
        denoise_kernel,
        "denoise",
        [
            ((fields, band_cells), F32),
            ((fields, band_cells), F32),
            ((fields, edge_cells), F32),
            ((fields, edge_cells), F32),
        ],
        scratch(
            [((diff_in.shape[1], cells), BF16), ((width_r, cells), BF16), ((width_d, cells), F32)]
            + hidden_d * 2 + taps_d + left_d
        ),
        flops=4 * 10**9,
    )(
        rows, noise_draw, skip, reg, pair_skip, pair_reg,
        outer_skip, outer_reg, diff_in, diff_skip, diff_mid, diff_out, embed,
    )
    pair_band = permute(send_pair, pair)
    next_band = permute(send_next, across)
    piece = ((fields, BAND, LANES), F32)
    own, send = call(average_kernel, "average", [piece, piece])(mean, band, pair_band, next_band)
    got = permute(send, other)
    (out,) = call(output_kernel, "output", [((1, 2, fields, BAND, LANES), F32)])(own, got)
    return out


def solution(mesh):
    return jax.shard_map(
        shards,
        mesh=mesh,
        in_specs=(P(None, None, "tile", None), P(None, None, "tile", None)) + (P(),) * 8,
        out_specs=P("segment", None, None, "tile", None),
        check_vma=False,
    )
```

time: 27.9 us -> 27.2 us (0.975)
  the two profiles are of different devices: /device:TPU:24 before, /device:TPU:0 now
where the time goes in v2:
time: 27.2 us; the launch traced here: 27 us
  Pallas kernels  11.8 us (43%)
  waiting for transfers between devices  7.6 us (28%)
  starting transfers between devices  6.12 us (22%)
  local copies, waits for them, and re-layouts  1.34 us (5%)
    ppermute x8, waiting for transfers between devices, permute(): return lax.ppermute(value, ('segment', 'tile'), edges)  7.6 us
    ppermute x8, starting transfers between devices, permute(): return lax.ppermute(value, ('segment', 'tile'), edges)  6.12 us
    pallas_call x1, Pallas kernels, shards(): call(denoise_kernel, 'denoise', [((fields, band_cells), F32), ((fields, b...  5.44 us
    pallas_call x1, Pallas kernels, shards(): call(regress_kernel, 'regress', [((inputs, cells), F32), ((width_r, band_...  4.1 us
    unnamed x20, local copies, waits for them, and re-layouts  1.34 us
    pallas_call x1, Pallas kernels, shards(): call(outer_kernel, 'outer', [((width_r, edge_cells), BF16), ((fields, ban...  1.28 us
    pallas_call x1, Pallas kernels, shards(): call(output_kernel, 'output', [((1, 2, fields, BAND, LANES), F32)])  0.61 us
  transfers between devices with their start and end apart: 8, of which 4 were waited for; matrix products, arithmetic and copies ran while one was open for 0% of the time, Pallas kernels for 6%

profile of v2, /device:TPU:0, one launch (start us, length us, event | category | flops | bytes accessed | tf_op | source)
XLA Modules:
  0.0 27.0 jit_solution(17612796420544167331)
XLA Ops:
  0.0 0.5 %collective-permute-start = (bf16[2,8,4,128]{3,2,1,0:T(4,128)(2,1)}, bf16[2,8,4,128]{3,2,1,0:T(4,128)(2,1)S(1)}, u32[]{:S(2)}, u32[]{:S(2)}) collective-permute-start(bf16[2,8,4,128]{3,2,1,0:T(4,128)(2,1)} %coarse_ref.1), channel_id=1, source_target_pairs={{0,1},{1,0},{2,3},{3,2},{4,5},{5,4},{6,7},{7,6},{8,9},{9,8},{10,11... | collective-permute-start | bytes 49160 | tf_op jit(solution)/shard_map/ppermute | solution.py:439
  0.5 2.5 %collective-permute-start.1 = (bf16[2,8,4,128]{3,2,1,0:T(4,128)(2,1)}, bf16[2,8,4,128]{3,2,1,0:T(4,128)(2,1)S(1)}, u32[]{:S(2)}, u32[]{:S(2)}) collective-permute-start(bf16[2,8,4,128]{3,2,1,0:T(4,128)(2,1)} %coarse_ref.1), channel_id=1, source_target_pairs={{0,16},{1,2},{2,1},{3,4},{4,3},{5,6},{6,5},{7,8},{8,7},{9,10},{10,... | collective-permute-start | bytes 49160 | tf_op jit(solution)/shard_map/ppermute | solution.py:439
  3.0 0.7 %copy-done.9 = f32[256]{0:T(256)S(1)} copy-done((f32[256]{0:T(256)S(1)}, f32[256]{0:T(256)}, u32[]{:S(2)}) %copy-start.9) | copy-done | bytes 1048
  3.7 0.1 prepare.1.embed_ref
  3.8 0.0 collective-permute-done.pair_ref
  3.8 0.6 %collective-permute-start.2 = (bf16[2,8,4,128]{3,2,1,0:T(4,128)(2,1)S(1)}, bf16[2,8,4,128]{3,2,1,0:T(4,128)(2,1)S(1)}, u32[]{:S(2)}, u32[]{:S(2)}) collective-permute-start(bf16[2,8,4,128]{3,2,1,0:T(4,128)(2,1)S(1)} %collective-permute-done.pair_ref), channel_id=1, source_target_pairs={{0,16},{1,2},{2,1},{3,4},{4,3},{5,6},{6,5},{7,8},{8,7},{9,10},{10,... | collective-permute-start | bytes 49160 | tf_op jit(solution)/shard_map/ppermute | solution.py:439
  4.4 0.6 %copy-done = bf16[2,192,1728]{2,1,0:T(8,128)(2,1)S(1)} copy-done((bf16[2,192,1728]{2,1,0:T(8,128)(2,1)S(1)}, bf16[2,192,1728]{2,1,0:T(8,128)(2,1)}, u32[]{:S(2)}) %copy-start) | copy-done | bytes 1327128
  5.0 0.0 copy-start.7
  5.0 0.3 %weights.1 = (bf16[192,72]{1,0:T(8,128)(2,1)S(1)}, bf16[2,192,1728]{2,1,0:T(8,128)(2,1)S(1)}, bf16[256,144]{1,0:T(8,128)(2,1)S(1)}, bf16[256,192]{1,0:T(8,128)(2,1)S(1)}) custom-call(f32[256,128]{1,0:T(8,128)S(1)} %prepare.1.embed_ref, bf16[72,192]{1,0:T(8,128)(2,1)S(1)} %bitcast.6, bf16[2,192,1728]{2,1,0:T(8,128)(2,1)S(1)} %copy-done, ...), custom_call_target="tpu_custom_call" | custom-call | flops 4000000000 | tf_op jit(solution)/shard_map/weights/pallas_call | solution.py:459
  5.3 2.2 %collective-permute-done.2.far_ref = bf16[2,8,4,128]{3,2,1,0:T(4,128)(2,1)S(1)} collective-permute-done((bf16[2,8,4,128]{3,2,1,0:T(4,128)(2,1)S(1)}, bf16[2,8,4,128]{3,2,1,0:T(4,128)(2,1)S(1)}, u32[]{:S(2)}, u32[]{:S(2)}) %collective-permute-start.2) | collective-permute-done | bytes 16416 | tf_op jit(solution)/shard_map/ppermute | solution.py:439
  7.6 4.1 %regress.1 = (f32[8,1024]{1,0:T(8,128)S(1)}, bf16[192,512]{1,0:T(8,128)(2,1)S(1)}, f32[4,1024]{1,0:T(4,128)S(1)}, bf16[192,256]{1,0:T(8,128)(2,1)S(1)}, f32[4,51...) custom-call(bf16[2,8,4,128]{3,2,1,0:T(4,128)(2,1)S(1)} %copy-done.6,, ...), custom_call_target="tpu_custom_call" | custom-call | flops 3000000000 | tf_op jit(solution)/shard_map/regress/pallas_call | solution.py:467
  11.7 0.0 collective-permute-start.3
  11.7 0.5 %collective-permute-start.4 = (f32[4,512]{1,0:T(4,128)S(1)}, f32[4,512]{1,0:T(4,128)S(1)}, u32[]{:S(2)}, u32[]{:S(2)}) collective-permute-start(f32[4,512]{1,0:T(4,128)S(1)} %get-tuple-element.48), channel_id=1, source_target_pairs={{0,1},{1,0},{2,3},{3,2},{4,5},{5,4},{6,7},{7,6},{8,9},{9,8},{10,11... | collective-permute-start | bytes 24584 | tf_op jit(solution)/shard_map/ppermute | solution.py:439
  12.2 1.3 %outer.1 = (bf16[192,256]{1,0:T(8,128)(2,1)S(1)}, f32[4,512]{1,0:T(4,128)S(1)}) custom-call(bf16[2,192,1728]{2,1,0:T(8,128)(2,1)S(1)} %get-tuple-element.43.reg_mid_ref, bf16[4,192]{1,0:T(4,128)(2,1)S(1)} %copy-done.7, f32[192,256]{1,0:T(8,128)S(1)} %get-tuple-element.49.refs_0_, f32[192,256]{1,0:T(8,128)S(1)} %get-tuple-element.50.refs_1_, ...), custom_call_target="tpu_custom_call" | custom-call | flops 1000000000 | tf_op jit(solution)/shard_map/outer/pallas_call | solution.py:483
  13.5 0.0 collective-permute-done.4.pair_reg_ref
  13.5 0.0 collective-permute-done.3.pair_skip_ref
  13.5 5.4 %denoise.1 = (f32[4,512]{1,0:T(4,128)S(1)}, f32[4,512]{1,0:T(4,128)S(1)}, f32[4,256]{1,0:T(4,128)S(1)}, f32[4,256]{1,0:T(4,128)S(1)}) custom-call(f32[8,1024]{1,0:T(8,128)S(1)} %get-tuple-element.44.rows_ref, f32[2,4,8,128]{3,2,1,0:T(8,128)S(1)} %copy-done.5, bf16[192,512]{1,0:T(8,128)(2,1)S(1)} %get-tuple-element.45.skip_ref, ...), custom_call_target="tpu_custom_call" | custom-call | flops 4000000000 | tf_op jit(solution)/shard_map/denoise/pallas_call | solution.py:490
  19.0 0.1 collective-permute-start.5
  19.0 0.9 %collective-permute-start.6 = (f32[4,256]{1,0:T(4,128)S(1)}, f32[4,256]{1,0:T(4,128)S(1)}, u32[]{:S(2)}, u32[]{:S(2)}) collective-permute-start(f32[4,256]{1,0:T(4,128)S(1)} %get-tuple-element.76), channel_id=1, source_target_pairs={{0,16},{1,2},{2,1},{3,4},{4,3},{5,6},{6,5},{7,8},{8,7},{9,10},{10,... | collective-permute-start | bytes 12296 | tf_op jit(solution)/shard_map/ppermute | solution.py:439
  20.0 0.1 collective-permute-done.5.pair_ref
  20.1 2.5 %collective-permute-done.6.next_ref = f32[4,256]{1,0:T(4,128)S(1)} collective-permute-done((f32[4,256]{1,0:T(4,128)S(1)}, f32[4,256]{1,0:T(4,128)S(1)}, u32[]{:S(2)}, u32[]{:S(2)}) %collective-permute-start.6) | collective-permute-done | bytes 4128 | tf_op jit(solution)/shard_map/ppermute | solution.py:439
  22.7 1.0 %collective-permute-start.7 = (f32[4,4,128]{2,1,0:T(4,128)S(1)}, f32[4,4,128]{2,1,0:T(4,128)S(1)}, u32[]{:S(2)}, u32[]{:S(2)}) collective-permute-start(f32[4,4,128]{2,1,0:T(4,128)S(1)} %get-tuple-element.78), channel_id=1, source_target_pairs={{0,16},{1,17},{2,18},{3,19},{4,20},{5,21},{6,22},{7,23},{8,24},{9,... | collective-permute-start | bytes 24584 | tf_op jit(solution)/shard_map/ppermute | solution.py:439
  23.7 2.7 %collective-permute-done.7.got_ref = f32[4,4,128]{2,1,0:T(4,128)S(1)} collective-permute-done((f32[4,4,128]{2,1,0:T(4,128)S(1)}, f32[4,4,128]{2,1,0:T(4,128)S(1)}, u32[]{:S(2)}, u32[]{:S(2)}) %collective-permute-start.7) | collective-permute-done | bytes 8224 | tf_op jit(solution)/shard_map/ppermute | solution.py:439
  26.4 0.6 %output.1 = f32[1,2,4,4,128]{4,3,2,1,0:T(4,128)} custom-call(f32[4,4,128]{2,1,0:T(4,128)S(1)} %get-tuple-element.77.own_ref, f32[4,4,128]{2,1,0:T(4,128)S(1)} %collective-permute-done.7.got_ref), custom_call_target="tpu_custom_call" | custom-call | tf_op jit(solution)/shard_map/output/pallas_call | solution.py:513
  (19 shorter events, 0.1 us)
Async XLA Ops:
  0.0 3.8 %collective-permute-start = (bf16[2,8,4,128]{3,2,1,0:T(4,128)(2,1)}, bf16[2,8,4,128]{3,2,1,0:T(4,128)(2,1)S(1)}, u32[]{:S(2)}, u32[]{:S(2)}) collective-permute-start(bf16[2,8,4,128]{3,2,1,0:T(4,128)(2,1)} %coarse_ref.1), channel_id=1, source_target_pairs={{0,1},{1,0},{2,3},{3,2},{4,5},{5,4},{6,7},{7,6},{8,9},{9,8},{10,11... | collective-permute-start | bytes 49160 | tf_op jit(solution)/shard_map/ppermute | solution.py:439
  0.5 4.9 %collective-permute-start.1 = (bf16[2,8,4,128]{3,2,1,0:T(4,128)(2,1)}, bf16[2,8,4,128]{3,2,1,0:T(4,128)(2,1)S(1)}, u32[]{:S(2)}, u32[]{:S(2)}) collective-permute-start(bf16[2,8,4,128]{3,2,1,0:T(4,128)(2,1)} %coarse_ref.1), channel_id=1, source_target_pairs={{0,16},{1,2},{2,1},{3,4},{4,3},{5,6},{6,5},{7,8},{8,7},{9,10},{10,... | collective-permute-start | bytes 49160 | tf_op jit(solution)/shard_map/ppermute | solution.py:439
  3.0 0.7 %copy-start.9 = (f32[256]{0:T(256)S(1)}, f32[256]{0:T(256)}, u32[]{:S(2)}) copy-start(f32[256]{0:T(256)} %param.19) | copy-start | bytes 3076
  3.7 1.3 %copy-start = (bf16[2,192,1728]{2,1,0:T(8,128)(2,1)S(1)}, bf16[2,192,1728]{2,1,0:T(8,128)(2,1)}, u32[]{:S(2)}) copy-start(bf16[2,192,1728]{2,1,0:T(8,128)(2,1)} %reg_mid_ref.1) | copy-start | bytes 3981316
  3.7 1.3 %copy-start.2 = (bf16[256,192]{0,1:T(8,128)(2,1)S(1)}, bf16[256,192]{0,1:T(8,128)(2,1)}, u32[]{:S(2)}) copy-start(bf16[256,192]{0,1:T(8,128)(2,1)} %param.16) | copy-start | bytes 294916
  3.7 1.3 %copy-start.3 = (bf16[256,144]{0,1:T(8,128)(2,1)S(1)}, bf16[256,144]{0,1:T(8,128)(2,1)}, u32[]{:S(2)}) copy-start(bf16[256,144]{0,1:T(8,128)(2,1)} %param.15) | copy-start | bytes 221188
  3.7 1.3 %copy-start.4 = (bf16[192,72]{0,1:T(8,128)(2,1)S(1)}, bf16[192,72]{0,1:T(8,128)(2,1)}, u32[]{:S(2)}) copy-start(bf16[192,72]{0,1:T(8,128)(2,1)} %param.12) | copy-start | bytes 82948
  3.8 3.8 %collective-permute-start.2 = (bf16[2,8,4,128]{3,2,1,0:T(4,128)(2,1)S(1)}, bf16[2,8,4,128]{3,2,1,0:T(4,128)(2,1)S(1)}, u32[]{:S(2)}, u32[]{:S(2)}) collective-permute-start(bf16[2,8,4,128]{3,2,1,0:T(4,128)(2,1)S(1)} %collective-permute-done.pair_ref), channel_id=1, source_target_pairs={{0,16},{1,2},{2,1},{3,4},{4,3},{5,6},{6,5},{7,8},{8,7},{9,10},{10,... | collective-permute-start | bytes 49160 | tf_op jit(solution)/shard_map/ppermute | solution.py:439
  5.0 2.6 %copy-start.6 = (bf16[2,8,4,128]{3,2,1,0:T(4,128)(2,1)S(1)}, bf16[2,8,4,128]{3,2,1,0:T(4,128)(2,1)}, u32[]{:S(2)}) copy-start(bf16[2,8,4,128]{3,2,1,0:T(4,128)(2,1)} %coarse_ref.1) | copy-start | bytes 49156
  5.0 2.6 %copy-start.7 = (bf16[4,192]{1,0:T(4,128)(2,1)S(1)}, bf16[4,192]{1,0:T(4,128)(2,1)}, u32[]{:S(2)}) copy-start(bf16[4,192]{1,0:T(4,128)(2,1)} %reg_out_ref.3) | copy-start | bytes 4612
  11.7 1.8 %collective-permute-start.3 = (bf16[192,256]{1,0:T(8,128)(2,1)S(1)}, bf16[192,256]{1,0:T(8,128)(2,1)S(1)}, u32[]{:S(2)}, u32[]{:S(2)}) collective-permute-start(bf16[192,256]{1,0:T(8,128)(2,1)S(1)} %get-tuple-element.47), channel_id=1, source_target_pairs={{0,1},{1,0},{2,3},{3,2},{4,5},{5,4},{6,7},{7,6},{8,9},{9,8},{10,11... | collective-permute-start | bytes 294920 | tf_op jit(solution)/shard_map/ppermute | solution.py:439
  11.7 1.8 %collective-permute-start.4 = (f32[4,512]{1,0:T(4,128)S(1)}, f32[4,512]{1,0:T(4,128)S(1)}, u32[]{:S(2)}, u32[]{:S(2)}) collective-permute-start(f32[4,512]{1,0:T(4,128)S(1)} %get-tuple-element.48), channel_id=1, source_target_pairs={{0,1},{1,0},{2,3},{3,2},{4,5},{5,4},{6,7},{7,6},{8,9},{9,8},{10,11... | collective-permute-start | bytes 24584 | tf_op jit(solution)/shard_map/ppermute | solution.py:439
  12.2 1.3 %copy-start.1 = (bf16[256,2304]{1,0:T(8,128)(2,1)S(1)}, bf16[256,2304]{1,0:T(8,128)(2,1)}, u32[]{:S(2)}) copy-start(bf16[256,2304]{1,0:T(8,128)(2,1)} %diff_mid_ref.1) | copy-start | bytes 3538948
  12.2 1.3 %copy-start.5 = (f32[2,4,8,128]{3,2,1,0:T(8,128)S(1)}, f32[2,4,8,128]{3,2,1,0:T(8,128)}, u32[]{:S(2)}) copy-start(f32[2,4,8,128]{3,2,1,0:T(8,128)} %noise_ref.1) | copy-start | bytes 98308
  12.2 1.3 %copy-start.8 = (bf16[4,256]{1,0:T(4,128)(2,1)S(1)}, bf16[4,256]{1,0:T(4,128)(2,1)}, u32[]{:S(2)}) copy-start(bf16[4,256]{1,0:T(4,128)(2,1)} %diff_out_ref.1) | copy-start | bytes 6148
  19.0 1.2 %collective-permute-start.5 = (f32[4,256]{1,0:T(4,128)S(1)}, f32[4,256]{1,0:T(4,128)S(1)}, u32[]{:S(2)}, u32[]{:S(2)}) collective-permute-start(f32[4,256]{1,0:T(4,128)S(1)} %get-tuple-element.75), channel_id=1, source_target_pairs={{0,1},{1,0},{2,3},{3,2},{4,5},{5,4},{6,7},{7,6},{8,9},{9,8},{10,11... | collective-permute-start | bytes 12296 | tf_op jit(solution)/shard_map/ppermute | solution.py:439
  19.0 3.6 %collective-permute-start.6 = (f32[4,256]{1,0:T(4,128)S(1)}, f32[4,256]{1,0:T(4,128)S(1)}, u32[]{:S(2)}, u32[]{:S(2)}) collective-permute-start(f32[4,256]{1,0:T(4,128)S(1)} %get-tuple-element.76), channel_id=1, source_target_pairs={{0,16},{1,2},{2,1},{3,4},{4,3},{5,6},{6,5},{7,8},{8,7},{9,10},{10,... | collective-permute-start | bytes 12296 | tf_op jit(solution)/shard_map/ppermute | solution.py:439
  22.7 3.7 %collective-permute-start.7 = (f32[4,4,128]{2,1,0:T(4,128)S(1)}, f32[4,4,128]{2,1,0:T(4,128)S(1)}, u32[]{:S(2)}, u32[]{:S(2)}) collective-permute-start(f32[4,4,128]{2,1,0:T(4,128)S(1)} %get-tuple-element.78), channel_id=1, source_target_pairs={{0,16},{1,17},{2,18},{3,19},{4,20},{5,21},{6,22},{7,23},{8,24},{9,... | collective-permute-start | bytes 24584 | tf_op jit(solution)/shard_map/ppermute | solution.py:439

commit v3 on v2

--- a/solution.py
+++ b/solution.py
@@ -117,17 +117,21 @@
         self.channels = hidden[0].shape[0]
         self.whole, self.rest = depths(self.channels)
 
-    def start(self, first_rows):
+    def start_steps(self, first_rows):
         norm = Norm(self.channels)
-        for k, ref in enumerate(self.hidden):
+
+        def step(k):
             chunk = first_rows(k * STEP)
-            ref[...] = chunk
+            self.hidden[k][...] = chunk
             norm.add(chunk)
-        self.scales = norm.scales()
-        if self.rest:
-            blank = jnp.zeros((self.rest, LANES), BF16)
-            self.left[0][: self.rest, :] = blank
-            self.left[-1][2 * self.rest :, :] = blank
+            if k == len(self.hidden) - 1:
+                self.scales = norm.scales()
+                if self.rest:
+                    blank = jnp.zeros((self.rest, LANES), BF16)
+                    self.left[0][: self.rest, :] = blank
+                    self.left[-1][2 * self.rest :, :] = blank
+
+        return [lambda k=k: step(k) for k in range(len(self.hidden))]
 
     def rows(self, row):
         return self.hidden[row // STEP][:, lanes(row % STEP)]
@@ -201,6 +205,14 @@
     embed_out[...] = jnp.broadcast_to(embed_ref[...], embed_out.shape[::-1]).T
 
 
+def six_rows_kernel(coarse_ref, pair_ref, mine_ref):
+    even, first, last = place()
+    sample = lax.axis_index("segment")
+    own, pair = ([ref[sample].astype(F32)[:, r, :] for r in range(BAND)] for ref in (coarse_ref, pair_ref))
+    for i, (low, high) in enumerate(zip(own + pair[:MARGIN], pair[MARGIN:] + own)):
+        mine_ref[:, lanes(i)] = jnp.where(even, low, high).astype(BF16)
+
+
 def weights_kernel(
     embed_ref, reg_in_ref, reg_mid_ref, diff_in_ref, diff_skip_ref,
     reg_in_out, reg_mid_out, diff_in_out, diff_skip_out,
@@ -213,18 +225,14 @@
         reg_mid_out[block] = packed(reg_mid_ref[block])
 
 
-def coarse_window(coarse_ref, pair_ref, next_ref, far_ref):
+def coarse_window(mine_ref, across_ref):
     even, first, last = place()
-    sample = lax.axis_index("segment")
-    own, pair, across, far = (
-        [ref[sample].astype(F32)[:, r, :] for r in range(BAND)]
-        for ref in (coarse_ref, pair_ref, next_ref, far_ref)
-    )
     alone = jnp.logical_or(jnp.logical_and(even, first), jnp.logical_and(jnp.logical_not(even), last))
-    across, far = ([jnp.where(alone, jnp.zeros_like(r), r) for r in rows] for rows in (across, far))
-    low = far[2:] + across + own + pair[:2]
-    high = pair[2:] + own + across + far[:2]
-    return even, [jnp.where(even, a, b) for a, b in zip(low, high)]
+    mine, across = (
+        [ref[:, lanes(i)].astype(F32) for i in range(BAND + MARGIN)] for ref in (mine_ref, across_ref)
+    )
+    across = [jnp.where(alone, jnp.zeros_like(r), r) for r in across]
+    return even, [jnp.where(even, a, b) for a, b in zip(across + mine, mine + across)]
 
 
 def own_rows(even, window):
@@ -232,11 +240,11 @@
 
 
 def regress_kernel(
-    coarse_ref, pair_ref, next_ref, far_ref, reg_in_ref, reg_mid_ref, reg_out_ref,
-    rows_ref, skip_ref, reg_ref, send_skip_ref, send_reg_ref, *refs,
+    mine_ref, across_ref, reg_in_ref, reg_mid_ref, reg_out_ref,
+    rows_ref, skip_ref, reg_ref, send_ref, *refs,
 ):
     taps_in_a, taps_in_b = refs[-2:]
-    even, window = coarse_window(coarse_ref, pair_ref, next_ref, far_ref)
+    even, window = coarse_window(mine_ref, across_ref)
     rows_a = own_rows(even, window)
     rows_b = [jnp.where(even, window[i], window[i + BAND]) for i in range(ROWS)]
     for r in range(ROWS):
@@ -250,34 +258,39 @@
     outer = Patch(*hidden_b, taps_out, left_out)
     own = Patch(refs[:half], refs[half : 2 * half], refs[2 * half : 2 * half + ROWS], refs[2 * half + ROWS :])
     reg_in = reg_in_ref[...]
-    for patch, rows, taps_in in ((own, rows_a, taps_in_a), (outer, rows_b, taps_in_b)):
-        input_taps(rows, taps_in)
-        patch.start(
+
+    def in_steps(patch, rows, taps_in):
+        steps = patch.start_steps(
             lambda r: jnp.dot(reg_in, taps_in[:, lanes(r, STEP)], preferred_element_type=F32)
         )
-
+        return [lambda: input_taps(rows, taps_in)] + steps + patch.act_steps()
+
+    run(in_steps(own, rows_a, taps_in_a))
+    outer_steps = in_steps(outer, rows_b, taps_in_b)
     for block in range(blocks):
         def weight():
             return reg_mid_ref[block]
 
-        if block == 0:
-            run(own.act_steps())
-        run(own.conv_steps(weight), outer.act_steps())
+        run(own.conv_steps(weight), outer_steps)
         if block < blocks - 1:
             run(outer.conv_steps(weight), own.act_steps())
+            outer_steps = outer.act_steps()
 
     for i in range(BAND):
         skip_ref[:, lanes(i)] = own.rows(MARGIN + i).astype(BF16)
+    width = skip_ref.shape[0]
     for i in range(MARGIN):
-        send_skip_ref[:, lanes(i)] = jnp.where(even, own.rows(4 + i), own.rows(2 + i)).astype(BF16)
+        send_ref[:width, lanes(i)] = jnp.where(even, own.rows(4 + i), own.rows(2 + i)).astype(BF16)
     reg = []
     for hidden in own.hidden:
         act = silu(hidden[...], [jnp.concatenate([s] * STEP, axis=1) for s in own.scales])
         reg.append(jnp.dot(reg_out_ref[...], act, preferred_element_type=F32))
     for k, part in enumerate(reg):
         reg_ref[:, lanes(k * STEP, STEP)] = part
-    for k in range(half // 2):
-        send_reg_ref[:, lanes(k * STEP, STEP)] = jnp.where(even, reg[half // 2 + k], reg[k])
+    parts = [jnp.where(even, reg[half // 2 + k], reg[k]) for k in range(half // 2)]
+    tops = [part.astype(BF16).astype(F32) for part in parts]
+    parts = tops + [part - top for part, top in zip(parts, tops)]
+    send_ref[width:, :] = jnp.concatenate(parts, axis=0).astype(BF16)
 
 
 def outer_kernel(reg_mid_ref, reg_out_ref, *refs):
@@ -300,7 +313,7 @@
 
 
 def denoise_kernel(
-    rows_ref, noise_ref, skip_ref, reg_ref, pair_skip_ref, pair_reg_ref,
+    rows_ref, noise_ref, skip_ref, reg_ref, pair_ref,
     outer_skip_ref, outer_reg_ref, diff_in_ref, diff_skip_ref, diff_mid_ref, diff_out_ref, embed_ref,
     mean_ref, band_ref, send_pair_ref, send_next_ref,
     taps_in, skips, base, *refs,
@@ -308,8 +321,12 @@
     even, first, last = place()
     coarse = [rows_ref[:, lanes(r)] for r in range(ROWS)]
     reg = [reg_ref[:, lanes(r)] for r in range(ROWS)]
-    up = [jnp.where(even, outer_reg_ref[:, lanes(i)], pair_reg_ref[:, lanes(i)]) for i in range(4)]
-    down = [jnp.where(even, pair_reg_ref[:, lanes(i)], outer_reg_ref[:, lanes(i)]) for i in range(4)]
+    width, fields = skip_ref.shape[0], reg_ref.shape[0]
+    parts = pair_ref[width:, :].astype(F32)
+    parts = parts[: 2 * fields] + parts[2 * fields :]
+    pair_reg = [parts[fields * (i // STEP) : fields * (i // STEP + 1), lanes(i % STEP)] for i in range(BAND)]
+    up = [jnp.where(even, outer_reg_ref[:, lanes(i)], pair_reg[i]) for i in range(4)]
+    down = [jnp.where(even, pair_reg[i], outer_reg_ref[:, lanes(i)]) for i in range(4)]
     mean = []
     for r in range(ROWS):
         both = 0.5 * (reg[r] + (up[r] if r < 4 else down[r - 4]))
@@ -325,8 +342,8 @@
         mean_ref[:, lanes(i)] = mean[MARGIN + i]
     mean = [m.astype(BF16).astype(F32) for m in mean]
     for i in range(2):
-        low = jnp.where(even, outer_skip_ref[:, lanes(i)], pair_skip_ref[:, lanes(i)])
-        high = jnp.where(even, pair_skip_ref[:, lanes(i)], outer_skip_ref[:, lanes(i)])
+        low = jnp.where(even, outer_skip_ref[:, lanes(i)], pair_ref[:width, lanes(i)])
+        high = jnp.where(even, pair_ref[:width, lanes(i)], outer_skip_ref[:, lanes(i)])
         skips[:, lanes(i)] = jnp.where(first, jnp.zeros_like(low), low)
         skips[:, lanes(6 + i)] = jnp.where(last, jnp.zeros_like(high), high)
     skips[:, lanes(MARGIN, BAND)] = skip_ref[...]
@@ -358,7 +375,7 @@
             fresh = jnp.dot(diff_in_ref[...], taps_in[:, lanes(r, STEP)], preferred_element_type=F32)
             return fresh + base[:, lanes(r, STEP)] + shift
 
-        patch.start(first_rows)
+        run(patch.start_steps(first_rows))
         acts = patch.act_steps()
         convs = patch.conv_steps(lambda: diff_mid_ref[...])
         for step in acts[: STEP + 1]:
@@ -453,9 +470,11 @@
     taps_cells = cells + 2 * LANES
 
     pair_coarse = permute(coarse, pair)
-    next_coarse = permute(coarse, across)
-    far_coarse = permute(pair_coarse, across)
     (embed,) = call(prepare_kernel, "prepare", [((width_d, LANES), F32)], flops=4 * 10**9)(noise_embed[None])
+    (mine,) = call(six_rows_kernel, "six_rows", [((inputs, band_cells + edge_cells), BF16)])(
+        coarse, pair_coarse
+    )
+    next_coarse = permute(mine, across)
     reg_in, reg_mid, diff_in, diff_skip = call(
         weights_kernel,
         "weights",
@@ -464,22 +483,20 @@
     )(embed, reg_in.T, reg_mid, diff_in.T, diff_skip.T)
     hidden_r, taps_r, left_r = patch_shapes(width_r)
     hidden_d, taps_d, left_d = patch_shapes(width_d)
-    rows, skip, reg, send_skip, send_reg, *outer = call(
+    rows, skip, reg, send, *outer = call(
         regress_kernel,
         "regress",
         [
             ((inputs, cells), F32),
             ((width_r, band_cells), BF16),
             ((fields, cells), F32),
-            ((width_r, edge_cells), BF16),
-            ((fields, band_cells), F32),
+            ((width_r + 2 * fields * BAND // MARGIN, edge_cells), BF16),
         ]
         + hidden_r + taps_r + left_r,
         scratch(hidden_r * 3 + taps_r + left_r + [((reg_in.shape[1], cells), BF16)] * 2),
         flops=3 * 10**9,
-    )(coarse, pair_coarse, next_coarse, far_coarse, reg_in, reg_mid, reg_out)
-    pair_skip = permute(send_skip, pair)
-    pair_reg = permute(send_reg, pair)
+    )(mine, next_coarse, reg_in, reg_mid, reg_out)
+    from_pair = permute(send, pair)
     outer_skip, outer_reg = call(
         outer_kernel,
         "outer",
@@ -502,7 +519,7 @@
         ),
         flops=4 * 10**9,
     )(
-        rows, noise_draw, skip, reg, pair_skip, pair_reg,
+        rows, noise_draw, skip, reg, from_pair,
         outer_skip, outer_reg, diff_in, diff_skip, diff_mid, diff_out, embed,
     )
     pair_band = permute(send_pair, pair)

time: 27.2 us -> 25.8 us (0.949)
  waiting for transfers between devices: 7.6 us -> 4.82 us
  starting transfers between devices: 6.12 us -> 7.66 us
  local copies, waits for them, and re-layouts: 1.34 us -> 1.06 us
    ppermute x8 -> x6, waiting for transfers between devices: 7.6 us -> 4.82 us  [permute(): return lax.ppermute(value, ('segment', 'tile'), edges)]
    ppermute x8 -> x6, starting transfers between devices: 6.12 us -> 7.66 us  [permute(): return lax.ppermute(value, ('segment', 'tile'), edges)]
    unnamed x20, local copies, waits for them, and re-layouts: 1.34 us -> 1.06 us
  transfers between devices with their start and end apart: 8 -> 6, of which waited for: 4 -> 4; matrix products, arithmetic and copies ran while one was open for 0% -> 0% of each run, Pallas kernels for 6% -> 6%
where the time goes in v3:
time: 25.8 us; the launch traced here: 25.6 us
  Pallas kernels  11.9 us (46%)
  starting transfers between devices  7.66 us (30%)
  waiting for transfers between devices  4.82 us (19%)
  local copies, waits for them, and re-layouts  1.06 us (4%)
    ppermute x6, starting transfers between devices, permute(): return lax.ppermute(value, ('segment', 'tile'), edges)  7.66 us
    pallas_call x1, Pallas kernels, shards(): call(denoise_kernel, 'denoise', [((fields, band_cells), F32), ((fields, b...  5.45 us
    ppermute x6, waiting for transfers between devices, permute(): return lax.ppermute(value, ('segment', 'tile'), edges)  4.82 us
    pallas_call x1, Pallas kernels, shards(): call(regress_kernel, 'regress', [((inputs, cells), F32), ((width_r, band_...  4.16 us
    pallas_call x1, Pallas kernels, shards(): call(outer_kernel, 'outer', [((width_r, edge_cells), BF16), ((fields, ban...  1.26 us
    unnamed x20, local copies, waits for them, and re-layouts  1.06 us
    pallas_call x1, Pallas kernels, shards(): call(output_kernel, 'output', [((1, 2, fields, BAND, LANES), F32)])  0.61 us
  transfers between devices with their start and end apart: 6, of which 4 were waited for; matrix products, arithmetic and copies ran while one was open for 0% of the time, Pallas kernels for 6%

profile of v3, /device:TPU:0, one launch (start us, length us, event | category | flops | bytes accessed | tf_op | source)
XLA Modules:
  0.0 25.6 jit_solution(2110967153870818783)
XLA Ops:
  0.0 0.5 %collective-permute-start = (bf16[2,8,4,128]{3,2,1,0:T(4,128)(2,1)}, bf16[2,8,4,128]{3,2,1,0:T(4,128)(2,1)S(1)}, u32[]{:S(2)}, u32[]{:S(2)}) collective-permute-start(bf16[2,8,4,128]{3,2,1,0:T(4,128)(2,1)} %coarse_ref.1), channel_id=1, source_target_pairs={{0,1},{1,0},{2,3},{3,2},{4,5},{5,4},{6,7},{7,6},{8,9},{9,8},{10,11... | collective-permute-start | bytes 49160 | tf_op jit(solution)/shard_map/ppermute | solution.py:456
  0.5 0.7 %copy-done.9 = f32[256]{0:T(256)S(1)} copy-done((f32[256]{0:T(256)S(1)}, f32[256]{0:T(256)}, u32[]{:S(2)}) %copy-start.9) | copy-done | bytes 1048
  1.1 0.0 copy-start.5
  1.2 0.1 prepare.1.embed_ref
  1.2 0.3 collective-permute-done.pair_ref
  1.5 0.3 %copy-done = bf16[2,8,4,128]{3,2,1,0:T(4,128)(2,1)S(1)} copy-done((bf16[2,8,4,128]{3,2,1,0:T(4,128)(2,1)S(1)}, bf16[2,8,4,128]{3,2,1,0:T(4,128)(2,1)}, u32[]{:S(2)}) %copy-start) | copy-done | bytes 16408
  1.9 2.6 %collective-permute-start.1 = (bf16[8,768]{1,0:T(8,128)(2,1)S(1)}, bf16[8,768]{1,0:T(8,128)(2,1)S(1)}, u32[]{:S(2)}, u32[]{:S(2)}) collective-permute-start(bf16[8,768]{1,0:T(8,128)(2,1)S(1)} %six_rows.1.mine_ref), channel_id=1, source_target_pairs={{0,16},{1,2},{2,1},{3,4},{4,3},{5,6},{6,5},{7,8},{8,7},{9,10},{10,... | collective-permute-start | bytes 36872 | tf_op jit(solution)/shard_map/ppermute | solution.py:456
  4.5 0.0 copy-done.1
  4.5 0.0 copy-start.7
  4.5 0.3 %weights.1 = (bf16[192,72]{1,0:T(8,128)(2,1)S(1)}, bf16[2,192,1728]{2,1,0:T(8,128)(2,1)S(1)}, bf16[256,144]{1,0:T(8,128)(2,1)S(1)}, bf16[256,192]{1,0:T(8,128)(2,1)S(1)}) custom-call(f32[256,128]{1,0:T(8,128)S(1)} %prepare.1.embed_ref, bf16[72,192]{1,0:T(8,128)(2,1)S(1)} %bitcast.6, bf16[2,192,1728]{2,1,0:T(8,128)(2,1)S(1)} %copy-done.1, ...), custom_call_target="tpu_custom_call" | custom-call | flops 4000000000 | tf_op jit(solution)/shard_map/weights/pallas_call | solution.py:478
  4.8 1.3 %collective-permute-done.1.across_ref = bf16[8,768]{1,0:T(8,128)(2,1)S(1)} collective-permute-done((bf16[8,768]{1,0:T(8,128)(2,1)S(1)}, bf16[8,768]{1,0:T(8,128)(2,1)S(1)}, u32[]{:S(2)}, u32[]{:S(2)}) %collective-permute-start.1) | collective-permute-done | bytes 12320 | tf_op jit(solution)/shard_map/ppermute | solution.py:456
  6.1 4.2 %regress.1 = (f32[8,1024]{1,0:T(8,128)S(1)}, bf16[192,512]{1,0:T(8,128)(2,1)S(1)}, f32[4,1024]{1,0:T(4,128)S(1)}, bf16[208,256]{1,0:T(8,128)(2,1)S(1)}, f32[192,...) custom-call(bf16[8,768]{1,0:T(8,128)(2,1)S(1)} %six_rows.1.mine_ref,, ...), custom_call_target="tpu_custom_call" | custom-call | flops 3000000000 | tf_op jit(solution)/shard_map/regress/pallas_call | solution.py:486
  10.3 0.1 collective-permute-start.2
  10.4 1.3 %outer.1 = (bf16[192,256]{1,0:T(8,128)(2,1)S(1)}, f32[4,512]{1,0:T(4,128)S(1)}) custom-call(bf16[2,192,1728]{2,1,0:T(8,128)(2,1)S(1)} %get-tuple-element.42.reg_mid_ref, bf16[4,192]{1,0:T(4,128)(2,1)S(1)} %copy-done.7, f32[192,256]{1,0:T(8,128)S(1)} %get-tuple-element.47.refs_0_, f32[192,256]{1,0:T(8,128)S(1)} %get-tuple-element.48.refs_1_, ...), custom_call_target="tpu_custom_call" | custom-call | flops 1000000000 | tf_op jit(solution)/shard_map/outer/pallas_call | solution.py:500
  11.7 0.0 collective-permute-done.2.pair_ref
  11.7 0.0 copy-done.6
  11.7 5.4 %denoise.1 = (f32[4,512]{1,0:T(4,128)S(1)}, f32[4,512]{1,0:T(4,128)S(1)}, f32[4,256]{1,0:T(4,128)S(1)}, f32[4,256]{1,0:T(4,128)S(1)}) custom-call(f32[8,1024]{1,0:T(8,128)S(1)} %get-tuple-element.43.rows_ref, f32[2,4,8,128]{3,2,1,0:T(8,128)S(1)} %copy-done.6, bf16[192,512]{1,0:T(8,128)(2,1)S(1)} %get-tuple-element.44.skip_ref, ...), custom_call_target="tpu_custom_call" | custom-call | flops 4000000000 | tf_op jit(solution)/shard_map/denoise/pallas_call | solution.py:507
  17.2 0.4 %collective-permute-start.3 = (f32[4,256]{1,0:T(4,128)S(1)}, f32[4,256]{1,0:T(4,128)S(1)}, u32[]{:S(2)}, u32[]{:S(2)}) collective-permute-start(f32[4,256]{1,0:T(4,128)S(1)} %get-tuple-element.73), channel_id=1, source_target_pairs={{0,1},{1,0},{2,3},{3,2},{4,5},{5,4},{6,7},{7,6},{8,9},{9,8},{10,11... | collective-permute-start | bytes 12296 | tf_op jit(solution)/shard_map/ppermute | solution.py:456
  17.6 2.0 %collective-permute-start.4 = (f32[4,256]{1,0:T(4,128)S(1)}, f32[4,256]{1,0:T(4,128)S(1)}, u32[]{:S(2)}, u32[]{:S(2)}) collective-permute-start(f32[4,256]{1,0:T(4,128)S(1)} %get-tuple-element.74), channel_id=1, source_target_pairs={{0,16},{1,2},{2,1},{3,4},{4,3},{5,6},{6,5},{7,8},{8,7},{9,10},{10,... | collective-permute-start | bytes 12296 | tf_op jit(solution)/shard_map/ppermute | solution.py:456
  19.6 0.0 collective-permute-done.3.pair_ref
  19.6 1.6 %collective-permute-done.4.next_ref = f32[4,256]{1,0:T(4,128)S(1)} collective-permute-done((f32[4,256]{1,0:T(4,128)S(1)}, f32[4,256]{1,0:T(4,128)S(1)}, u32[]{:S(2)}, u32[]{:S(2)}) %collective-permute-start.4) | collective-permute-done | bytes 4128 | tf_op jit(solution)/shard_map/ppermute | solution.py:456
  21.2 2.1 %collective-permute-start.5 = (f32[4,4,128]{2,1,0:T(4,128)S(1)}, f32[4,4,128]{2,1,0:T(4,128)S(1)}, u32[]{:S(2)}, u32[]{:S(2)}) collective-permute-start(f32[4,4,128]{2,1,0:T(4,128)S(1)} %get-tuple-element.76), channel_id=1, source_target_pairs={{0,16},{1,17},{2,18},{3,19},{4,20},{5,21},{6,22},{7,23},{8,24},{9,... | collective-permute-start | bytes 24584 | tf_op jit(solution)/shard_map/ppermute | solution.py:456
  23.3 1.6 %collective-permute-done.5.got_ref = f32[4,4,128]{2,1,0:T(4,128)S(1)} collective-permute-done((f32[4,4,128]{2,1,0:T(4,128)S(1)}, f32[4,4,128]{2,1,0:T(4,128)S(1)}, u32[]{:S(2)}, u32[]{:S(2)}) %collective-permute-start.5) | collective-permute-done | bytes 8224 | tf_op jit(solution)/shard_map/ppermute | solution.py:456
  24.9 0.6 %output.1 = f32[1,2,4,4,128]{4,3,2,1,0:T(4,128)} custom-call(f32[4,4,128]{2,1,0:T(4,128)S(1)} %get-tuple-element.75.own_ref, f32[4,4,128]{2,1,0:T(4,128)S(1)} %collective-permute-done.5.got_ref), custom_call_target="tpu_custom_call" | custom-call | tf_op jit(solution)/shard_map/output/pallas_call | solution.py:530
  (16 shorter events, 0.1 us)
Async XLA Ops:
  0.0 1.5 %collective-permute-start = (bf16[2,8,4,128]{3,2,1,0:T(4,128)(2,1)}, bf16[2,8,4,128]{3,2,1,0:T(4,128)(2,1)S(1)}, u32[]{:S(2)}, u32[]{:S(2)}) collective-permute-start(bf16[2,8,4,128]{3,2,1,0:T(4,128)(2,1)} %coarse_ref.1), channel_id=1, source_target_pairs={{0,1},{1,0},{2,3},{3,2},{4,5},{5,4},{6,7},{7,6},{8,9},{9,8},{10,11... | collective-permute-start | bytes 49160 | tf_op jit(solution)/shard_map/ppermute | solution.py:456
  0.5 0.7 %copy-start.9 = (f32[256]{0:T(256)S(1)}, f32[256]{0:T(256)}, u32[]{:S(2)}) copy-start(f32[256]{0:T(256)} %param.19) | copy-start | bytes 3076
  1.1 0.7 %copy-start = (bf16[2,8,4,128]{3,2,1,0:T(4,128)(2,1)S(1)}, bf16[2,8,4,128]{3,2,1,0:T(4,128)(2,1)}, u32[]{:S(2)}) copy-start(bf16[2,8,4,128]{3,2,1,0:T(4,128)(2,1)} %coarse_ref.1) | copy-start | bytes 49156
  1.1 3.3 %copy-start.1 = (bf16[2,192,1728]{2,1,0:T(8,128)(2,1)S(1)}, bf16[2,192,1728]{2,1,0:T(8,128)(2,1)}, u32[]{:S(2)}) copy-start(bf16[2,192,1728]{2,1,0:T(8,128)(2,1)} %reg_mid_ref.1) | copy-start | bytes 3981316
  1.1 3.3 %copy-start.3 = (bf16[256,192]{0,1:T(8,128)(2,1)S(1)}, bf16[256,192]{0,1:T(8,128)(2,1)}, u32[]{:S(2)}) copy-start(bf16[256,192]{0,1:T(8,128)(2,1)} %param.16) | copy-start | bytes 294916
  1.1 3.3 %copy-start.4 = (bf16[256,144]{0,1:T(8,128)(2,1)S(1)}, bf16[256,144]{0,1:T(8,128)(2,1)}, u32[]{:S(2)}) copy-start(bf16[256,144]{0,1:T(8,128)(2,1)} %param.15) | copy-start | bytes 221188
  1.1 3.3 %copy-start.5 = (bf16[192,72]{0,1:T(8,128)(2,1)S(1)}, bf16[192,72]{0,1:T(8,128)(2,1)}, u32[]{:S(2)}) copy-start(bf16[192,72]{0,1:T(8,128)(2,1)} %param.12) | copy-start | bytes 82948
  1.9 4.3 %collective-permute-start.1 = (bf16[8,768]{1,0:T(8,128)(2,1)S(1)}, bf16[8,768]{1,0:T(8,128)(2,1)S(1)}, u32[]{:S(2)}, u32[]{:S(2)}) collective-permute-start(bf16[8,768]{1,0:T(8,128)(2,1)S(1)} %six_rows.1.mine_ref), channel_id=1, source_target_pairs={{0,16},{1,2},{2,1},{3,4},{4,3},{5,6},{6,5},{7,8},{8,7},{9,10},{10,... | collective-permute-start | bytes 36872 | tf_op jit(solution)/shard_map/ppermute | solution.py:456
  4.5 1.7 %copy-start.7 = (bf16[4,192]{1,0:T(4,128)(2,1)S(1)}, bf16[4,192]{1,0:T(4,128)(2,1)}, u32[]{:S(2)}) copy-start(bf16[4,192]{1,0:T(4,128)(2,1)} %reg_out_ref.3) | copy-start | bytes 4612
  10.3 1.4 %collective-permute-start.2 = (bf16[208,256]{1,0:T(8,128)(2,1)S(1)}, bf16[208,256]{1,0:T(8,128)(2,1)S(1)}, u32[]{:S(2)}, u32[]{:S(2)}) collective-permute-start(bf16[208,256]{1,0:T(8,128)(2,1)S(1)} %get-tuple-element.46), channel_id=1, source_target_pairs={{0,1},{1,0},{2,3},{3,2},{4,5},{5,4},{6,7},{7,6},{8,9},{9,8},{10,11... | collective-permute-start | bytes 319496 | tf_op jit(solution)/shard_map/ppermute | solution.py:456
  10.4 1.3 %copy-start.2 = (bf16[256,2304]{1,0:T(8,128)(2,1)S(1)}, bf16[256,2304]{1,0:T(8,128)(2,1)}, u32[]{:S(2)}) copy-start(bf16[256,2304]{1,0:T(8,128)(2,1)} %diff_mid_ref.1) | copy-start | bytes 3538948
  10.4 1.3 %copy-start.6 = (f32[2,4,8,128]{3,2,1,0:T(8,128)S(1)}, f32[2,4,8,128]{3,2,1,0:T(8,128)}, u32[]{:S(2)}) copy-start(f32[2,4,8,128]{3,2,1,0:T(8,128)} %noise_ref.1) | copy-start | bytes 98308
  10.4 1.3 %copy-start.8 = (bf16[4,256]{1,0:T(4,128)(2,1)S(1)}, bf16[4,256]{1,0:T(4,128)(2,1)}, u32[]{:S(2)}) copy-start(bf16[4,256]{1,0:T(4,128)(2,1)} %diff_out_ref.1) | copy-start | bytes 6148
  17.2 2.4 %collective-permute-start.3 = (f32[4,256]{1,0:T(4,128)S(1)}, f32[4,256]{1,0:T(4,128)S(1)}, u32[]{:S(2)}, u32[]{:S(2)}) collective-permute-start(f32[4,256]{1,0:T(4,128)S(1)} %get-tuple-element.73), channel_id=1, source_target_pairs={{0,1},{1,0},{2,3},{3,2},{4,5},{5,4},{6,7},{7,6},{8,9},{9,8},{10,11... | collective-permute-start | bytes 12296 | tf_op jit(solution)/shard_map/ppermute | solution.py:456
  17.6 3.6 %collective-permute-start.4 = (f32[4,256]{1,0:T(4,128)S(1)}, f32[4,256]{1,0:T(4,128)S(1)}, u32[]{:S(2)}, u32[]{:S(2)}) collective-permute-start(f32[4,256]{1,0:T(4,128)S(1)} %get-tuple-element.74), channel_id=1, source_target_pairs={{0,16},{1,2},{2,1},{3,4},{4,3},{5,6},{6,5},{7,8},{8,7},{9,10},{10,... | collective-permute-start | bytes 12296 | tf_op jit(solution)/shard_map/ppermute | solution.py:456
  21.2 3.7 %collective-permute-start.5 = (f32[4,4,128]{2,1,0:T(4,128)S(1)}, f32[4,4,128]{2,1,0:T(4,128)S(1)}, u32[]{:S(2)}, u32[]{:S(2)}) collective-permute-start(f32[4,4,128]{2,1,0:T(4,128)S(1)} %get-tuple-element.76), channel_id=1, source_target_pairs={{0,16},{1,17},{2,18},{3,19},{4,20},{5,21},{6,22},{7,23},{8,24},{9,... | collective-permute-start | bytes 24584 | tf_op jit(solution)/shard_map/ppermute | solution.py:456

commit v4 on v3

--- a/solution.py
+++ b/solution.py
@@ -28,20 +28,19 @@
 
 
 def col_shifts(chunk):
-    index = jnp.int16 if chunk.dtype == BF16 else jnp.int32
-    lane = lax.broadcasted_iota(index, chunk.shape, 1)
+    lane = lax.broadcasted_iota(jnp.int32, chunk.shape, 1)
     zero = jnp.zeros_like(chunk)
     before = jnp.where(lane == 0, zero, pltpu.roll(chunk, 1, 1))
     after = jnp.where(lane == LANES - 1, zero, pltpu.roll(chunk, LANES - 1, 1))
     return before, chunk, after
 
 
-def group_total(part):
+def group_total(part, size):
     channels = part.shape[0]
-    size = channels // GROUPS
     if size == 8:
-        total = jnp.sum(part.reshape(GROUPS, 8, LANES), axis=(1, 2), keepdims=True)
-        return jnp.broadcast_to(total, (GROUPS, 8, LANES)).reshape(channels, LANES)
+        tiles = (channels // 8, 8, LANES)
+        total = jnp.sum(part.reshape(tiles), axis=(1, 2), keepdims=True)
+        return jnp.broadcast_to(total, tiles).reshape(channels, LANES)
     blocks = channels // 24
     tiles = part.reshape(blocks, 3, 8, LANES)
     row = lax.broadcasted_iota(jnp.int32, (blocks, 8, LANES), 1)
@@ -63,14 +62,14 @@
 
 
 class Norm:
-    def __init__(self, channels):
-        self.size = channels // GROUPS * LANES
+    def __init__(self, size):
+        self.size = size
         self.shift = None
 
     def add(self, chunk):
         rows = [chunk[:, lanes(r)] for r in range(STEP)]
         if self.shift is None:
-            self.shift = group_total(sum(rows[1:], rows[0])) * (1.0 / (STEP * self.size))
+            self.shift = group_total(sum(rows[1:], rows[0]), self.size) * (1.0 / (STEP * self.size * LANES))
             self.first = self.second = jnp.zeros_like(self.shift)
         for row in rows:
             away = row - self.shift
@@ -78,16 +77,16 @@
             self.second = self.second + away * away
 
     def scales(self):
-        share = 1.0 / (ROWS * self.size)
-        mean = group_total(self.first) * share
-        square = group_total(self.second) * share
+        share = 1.0 / (ROWS * self.size * LANES)
+        mean = group_total(self.first, self.size) * share
+        square = group_total(self.second, self.size) * share
         return self.shift + mean, 0.5 * lax.rsqrt(square - mean * mean + 1e-5)
 
 
 def silu(rows, scales):
     centre, half = scales
     v = (rows - centre) * half
-    return (v + v * jnp.tanh(v)).astype(BF16)
+    return v + v * jnp.tanh(v)
 
 
 def depths(channels):
@@ -118,7 +117,7 @@
         self.whole, self.rest = depths(self.channels)
 
     def start_steps(self, first_rows):
-        norm = Norm(self.channels)
+        norm = Norm(self.channels // GROUPS)
 
         def step(k):
             chunk = first_rows(k * STEP)
@@ -137,7 +136,8 @@
         return self.hidden[row // STEP][:, lanes(row % STEP)]
 
     def store(self, row):
-        shifts = jnp.concatenate(col_shifts(silu(self.rows(row), self.scales)), axis=0)
+        pieces = col_shifts(silu(self.rows(row), self.scales))
+        shifts = jnp.concatenate([piece.astype(BF16) for piece in pieces], axis=0)
         self.taps[row][...] = shifts[: self.whole]
         if self.rest:
             for a in range(3):
@@ -148,7 +148,7 @@
         return [lambda r=r: self.store(r) for r in range(ROWS)]
 
     def conv_steps(self, weight):
-        norm = Norm(self.channels)
+        norm = Norm(self.channels // GROUPS)
         source, target = self.hidden, self.hidden_next
 
         def tap_row(r):
@@ -173,6 +173,77 @@
         return [lambda k=k: step(k) for k in range(len(source))]
 
 
+class SplitPatch:
+    taps_order = [(a, b) for a in range(3) for b in range(3)]
+
+    def __init__(self, hidden, taps, size):
+        self.hidden, self.taps, self.size = hidden, taps, size
+        self.part = hidden[0][0].shape[0]
+        self.scales = [None, None]
+
+    def columns(self, p):
+        return slice(p * self.part, (p + 1) * self.part)
+
+    def start_steps(self, p, first_rows):
+        norm = Norm(self.size)
+
+        def step(k):
+            chunk = first_rows(self.columns(p), k * STEP)
+            self.hidden[p][k][...] = chunk
+            norm.add(chunk)
+            if k == ROWS // STEP - 1:
+                self.scales[p] = norm.scales()
+
+        return [lambda k=k: step(k) for k in range(ROWS // STEP)]
+
+    def store(self, p, row):
+        chunk = silu(self.hidden[p][row // STEP][:, lanes(row % STEP)], self.scales[p])
+        for b, piece in enumerate(col_shifts(chunk)):
+            self.taps[p][row][self.columns(b), :] = piece.astype(BF16)
+
+    def act_steps(self, p):
+        return [lambda r=r: self.store(p, r) for r in range(ROWS)]
+
+    def product(self, weight_ref, outs, taps, k):
+        first = k * STEP
+        weights, pieces = [], []
+        for p, a, b in taps:
+            at = ((3 * a + b) * 2 + p) * self.part
+            weights.append(weight_ref[outs, at : at + self.part])
+            rows = [first + i + a - 1 for i in range(STEP)]
+            blank = jnp.zeros((self.part, LANES), BF16)
+            pieces.append(
+                jnp.concatenate(
+                    [self.taps[p][r][self.columns(b), :] if 0 <= r < ROWS else blank for r in rows], axis=1
+                )
+            )
+        return jnp.dot(
+            jnp.concatenate(weights, axis=1), jnp.concatenate(pieces, axis=0), preferred_element_type=F32
+        )
+
+    def first_steps(self, weight_ref):
+        def step(k):
+            taps = [(0, a, b) for a, b in self.taps_order[:-1]]
+            added = self.product(weight_ref, slice(0, 2 * self.part), taps, k)
+            for p in range(2):
+                self.hidden[p][k][...] += added[self.columns(p)]
+
+        return [lambda k=k: step(k) for k in range(ROWS // STEP)]
+
+    def last_steps(self, weight_ref, p):
+        norm = Norm(self.size)
+
+        def step(k):
+            taps = [(1, a, b) for a, b in self.taps_order] + [(0, *self.taps_order[-1])]
+            chunk = self.hidden[p][k][...] + self.product(weight_ref, self.columns(p), taps, k)
+            self.hidden[p][k][...] = chunk
+            norm.add(chunk)
+            if k == ROWS // STEP - 1:
+                self.scales[p] = norm.scales()
+
+        return [lambda k=k: step(k) for k in range(ROWS // STEP)]
+
+
 def run(*columns):
     longest = max(len(c) for c in columns)
     done = [0] * len(columns)
@@ -184,10 +255,11 @@
 
 
 def input_taps(rows, out_ref):
-    if rows[0].shape[0] % 16 == 0:
-        rows = [row.astype(BF16) for row in rows]
     shifted = [col_shifts(row) for row in rows]
     blank = jnp.zeros_like(rows[0])
+    if rows[0].shape[0] % 16 == 0:
+        shifted = [[piece.astype(BF16) for piece in pieces] for pieces in shifted]
+        blank = blank.astype(BF16)
     for i in range(ROWS):
         pieces = []
         for a in range(3):
@@ -283,11 +355,12 @@
         send_ref[:width, lanes(i)] = jnp.where(even, own.rows(4 + i), own.rows(2 + i)).astype(BF16)
     reg = []
     for hidden in own.hidden:
-        act = silu(hidden[...], [jnp.concatenate([s] * STEP, axis=1) for s in own.scales])
+        act = silu(hidden[...], [jnp.concatenate([s] * STEP, axis=1) for s in own.scales]).astype(BF16)
         reg.append(jnp.dot(reg_out_ref[...], act, preferred_element_type=F32))
     for k, part in enumerate(reg):
         reg_ref[:, lanes(k * STEP, STEP)] = part
     parts = [jnp.where(even, reg[half // 2 + k], reg[k]) for k in range(half // 2)]
+    parts = [part[:, lanes(i, MARGIN)] for part in parts for i in range(0, STEP, MARGIN)]
     tops = [part.astype(BF16).astype(F32) for part in parts]
     parts = tops + [part - top for part, top in zip(parts, tops)]
     send_ref[width:, :] = jnp.concatenate(parts, axis=0).astype(BF16)
@@ -308,7 +381,7 @@
     for k in range(half // 2):
         rows = jnp.where(even, outer.hidden[half // 2 + k][...], outer.hidden[k][...])
         outer_reg_ref[:, lanes(k * STEP, STEP)] = jnp.dot(
-            reg_out_ref[...], silu(rows, scales), preferred_element_type=F32
+            reg_out_ref[...], silu(rows, scales).astype(BF16), preferred_element_type=F32
         )
 
 
@@ -324,7 +397,7 @@
     width, fields = skip_ref.shape[0], reg_ref.shape[0]
     parts = pair_ref[width:, :].astype(F32)
     parts = parts[: 2 * fields] + parts[2 * fields :]
-    pair_reg = [parts[fields * (i // STEP) : fields * (i // STEP + 1), lanes(i % STEP)] for i in range(BAND)]
+    pair_reg = [parts[fields * (i // MARGIN) : fields * (i // MARGIN + 1), lanes(i % MARGIN)] for i in range(BAND)]
     up = [jnp.where(even, outer_reg_ref[:, lanes(i)], pair_reg[i]) for i in range(4)]
     down = [jnp.where(even, pair_reg[i], outer_reg_ref[:, lanes(i)]) for i in range(4)]
     mean = []
@@ -351,7 +424,11 @@
     noise = noise_ref[lax.axis_index("segment")]
     initial = [sigma_high * noise[:, r, :] for r in range(ROWS)]
     half = ROWS // STEP
-    patch = Patch(refs[:half], refs[half : 2 * half], refs[2 * half : 2 * half + ROWS], refs[2 * half + ROWS :])
+    patch = SplitPatch(
+        (refs[:half], refs[half : 2 * half]),
+        (refs[2 * half : 2 * half + ROWS], refs[2 * half + ROWS :]),
+        diff_mid_ref.shape[0] // GROUPS,
+    )
 
     def denoise(current, sigma_now):
         total_var = sigma_now * sigma_now + sigma_data * sigma_data
@@ -367,30 +444,28 @@
         )
         shift = jnp.concatenate([(math.log(sigma_now) / 4.0) * embed] * STEP, axis=1)
 
-        def first_rows(r):
+        def first_rows(outs, r):
             if sigma_now == sigma_high:
-                base[:, lanes(r, STEP)] = jnp.dot(
-                    diff_skip_ref[...], skips[:, lanes(r, STEP)], preferred_element_type=F32
+                base[outs, lanes(r, STEP)] = jnp.dot(
+                    diff_skip_ref[outs, :], skips[:, lanes(r, STEP)], preferred_element_type=F32
                 )
-            fresh = jnp.dot(diff_in_ref[...], taps_in[:, lanes(r, STEP)], preferred_element_type=F32)
-            return fresh + base[:, lanes(r, STEP)] + shift
-
-        run(patch.start_steps(first_rows))
-        acts = patch.act_steps()
-        convs = patch.conv_steps(lambda: diff_mid_ref[...])
-        for step in acts[: STEP + 1]:
-            step()
-        acts = acts[STEP + 1 :]
-        for step in convs:
-            step()
-            for _ in range(min(STEP, len(acts))):
-                acts.pop(0)()
-        result = []
-        scales = [jnp.concatenate([s] * STEP, axis=1) for s in patch.scales]
-        for k, ref in enumerate(patch.hidden):
-            out = jnp.dot(diff_out_ref[...], silu(ref[...], scales), preferred_element_type=F32)
-            for i in range(STEP):
-                result.append(skip_coef * current[k * STEP + i] + out_coef * out[:, lanes(i)])
+            fresh = jnp.dot(diff_in_ref[outs, :], taps_in[:, lanes(r, STEP)], preferred_element_type=F32)
+            return fresh + base[outs, lanes(r, STEP)] + shift[outs]
+
+        run(patch.start_steps(0, first_rows))
+        run(patch.start_steps(1, first_rows))
+        run(patch.act_steps(0))
+        run(patch.act_steps(1))
+        run(patch.first_steps(diff_mid_ref))
+        run(patch.last_steps(diff_mid_ref, 0))
+        run(patch.last_steps(diff_mid_ref, 1))
+        scales = [[jnp.concatenate([s] * STEP, axis=1) for s in part] for part in patch.scales]
+        acts = []
+        for k in range(half):
+            pieces = [silu(patch.hidden[p][k][...], scales[p]).astype(BF16) for p in range(2)]
+            acts.append(jnp.concatenate(pieces, axis=0))
+        outs = jnp.dot(diff_out_ref[...], jnp.concatenate(acts, axis=1), preferred_element_type=F32)
+        result = [skip_coef * current[r] + out_coef * outs[:, lanes(r)] for r in range(ROWS)]
         return result
 
     denoised = denoise(initial, sigma_high)
@@ -405,20 +480,23 @@
         send_next_ref[:, lanes(i)] = jnp.where(even, final[i], final[6 + i])
 
 
-def average_kernel(mean_ref, band_ref, pair_ref, next_ref, own_ref, send_ref):
+def pair_average_kernel(band_ref, pair_ref, part_ref):
+    even, first, last = place()
+    for i in range(BAND):
+        here = band_ref[:, lanes(i)]
+        both = 0.5 * (here + pair_ref[:, lanes(i % MARGIN)])
+        part_ref[:, lanes(i)] = jnp.where(even if i >= MARGIN else jnp.logical_not(even), both, here)
+
+
+def average_kernel(mean_ref, part_ref, next_ref, own_ref, send_ref):
     even, first, last = place()
     lower = lax.axis_index("segment") == 0
     for i in range(BAND):
-        here = band_ref[:, lanes(i)]
+        here = part_ref[:, lanes(i)]
         mean = mean_ref[:, lanes(i)]
-        j = i % MARGIN
-        if i < MARGIN:
-            other = jnp.where(even, next_ref[:, lanes(j)], pair_ref[:, lanes(j)])
-            alone = first
-        else:
-            other = jnp.where(even, pair_ref[:, lanes(j)], next_ref[:, lanes(j)])
-            alone = last
-        value = jnp.where(alone, here, 0.5 * (here + other)) + mean.astype(BF16).astype(F32)
+        both = 0.5 * (here + next_ref[:, lanes(i % MARGIN)])
+        done, ends = (jnp.logical_not(even), first) if i < MARGIN else (even, last)
+        value = jnp.where(jnp.logical_or(done, ends), here, both) + mean.astype(BF16).astype(F32)
         own_ref[:, i, :] = jnp.where(lower, mean, value)
         send_ref[:, i, :] = jnp.where(lower, value, mean)
 
@@ -482,7 +560,8 @@
         flops=4 * 10**9,
     )(embed, reg_in.T, reg_mid, diff_in.T, diff_skip.T)
     hidden_r, taps_r, left_r = patch_shapes(width_r)
-    hidden_d, taps_d, left_d = patch_shapes(width_d)
+    hidden_d = [((width_d // 2, STEP * LANES), F32)] * (2 * ROWS // STEP)
+    taps_d = [((3 * width_d // 2, LANES), BF16)] * (2 * ROWS)
     rows, skip, reg, send, *outer = call(
         regress_kernel,
         "regress",
@@ -515,7 +594,7 @@
         ],
         scratch(
             [((diff_in.shape[1], cells), BF16), ((width_r, cells), BF16), ((width_d, cells), F32)]
-            + hidden_d * 2 + taps_d + left_d
+            + hidden_d + taps_d
         ),
         flops=4 * 10**9,
     )(
@@ -525,7 +604,10 @@
     pair_band = permute(send_pair, pair)
     next_band = permute(send_next, across)
     piece = ((fields, BAND, LANES), F32)
-    own, send = call(average_kernel, "average", [piece, piece])(mean, band, pair_band, next_band)
+    (part,) = call(pair_average_kernel, "pair_average", [((fields, band_cells), F32)], flops=2 * 10**9)(
+        band, pair_band
+    )
+    own, send = call(average_kernel, "average", [piece, piece])(mean, part, next_band)
     got = permute(send, other)
     (out,) = call(output_kernel, "output", [((1, 2, fields, BAND, LANES), F32)])(own, got)
     return out

time: 25.8 us -> 25.5 us (0.988)
    pallas_call x1, Pallas kernels: 5.45 us -> 5.14 us  [shards(): call(denoise_kernel, 'denoise', [((fields, band_cells), F32), ((fields, b...]
  transfers between devices with their start and end apart: 6 -> 6, of which waited for: 4 -> 4; matrix products, arithmetic and copies ran while one was open for 0% -> 0% of each run, Pallas kernels for 6% -> 7%
where the time goes in v4:
time: 25.5 us; the launch traced here: 25.3 us
  Pallas kernels  11.7 us (46%)
  starting transfers between devices  7.67 us (30%)
  waiting for transfers between devices  4.8 us (19%)
  local copies, waits for them, and re-layouts  1.06 us (4%)
    ppermute x6, starting transfers between devices, permute(): return lax.ppermute(value, ('segment', 'tile'), edges)  7.67 us
    pallas_call x1, Pallas kernels, shards(): call(denoise_kernel, 'denoise', [((fields, band_cells), F32), ((fields, b...  5.14 us
    ppermute x6, waiting for transfers between devices, permute(): return lax.ppermute(value, ('segment', 'tile'), edges)  4.8 us
    pallas_call x1, Pallas kernels, shards(): call(regress_kernel, 'regress', [((inputs, cells), F32), ((width_r, band_...  4.21 us
    pallas_call x1, Pallas kernels, shards(): call(outer_kernel, 'outer', [((width_r, edge_cells), BF16), ((fields, ban...  1.27 us
    unnamed x20, local copies, waits for them, and re-layouts  1.06 us
    pallas_call x1, Pallas kernels, shards(): call(output_kernel, 'output', [((1, 2, fields, BAND, LANES), F32)])  0.61 us
  transfers between devices with their start and end apart: 6, of which 4 were waited for; matrix products, arithmetic and copies ran while one was open for 0% of the time, Pallas kernels for 7%

profile of v4, /device:TPU:0, one launch (start us, length us, event | category | flops | bytes accessed | tf_op | source)
XLA Modules:
  0.0 25.3 jit_solution(11630165604568489950)
XLA Ops:
  0.0 0.5 %collective-permute-start = (bf16[2,8,4,128]{3,2,1,0:T(4,128)(2,1)}, bf16[2,8,4,128]{3,2,1,0:T(4,128)(2,1)S(1)}, u32[]{:S(2)}, u32[]{:S(2)}) collective-permute-start(bf16[2,8,4,128]{3,2,1,0:T(4,128)(2,1)} %coarse_ref.1), channel_id=1, source_target_pairs={{0,1},{1,0},{2,3},{3,2},{4,5},{5,4},{6,7},{7,6},{8,9},{9,8},{10,11... | collective-permute-start | bytes 49160 | tf_op jit(solution)/shard_map/ppermute | solution.py:534
  0.5 0.7 %copy-done.9 = f32[256]{0:T(256)S(1)} copy-done((f32[256]{0:T(256)S(1)}, f32[256]{0:T(256)}, u32[]{:S(2)}) %copy-start.9) | copy-done | bytes 1048
  1.2 0.1 prepare.1.embed_ref
  1.2 0.3 %collective-permute-done.pair_ref = bf16[2,8,4,128]{3,2,1,0:T(4,128)(2,1)S(1)} collective-permute-done((bf16[2,8,4,128]{3,2,1,0:T(4,128)(2,1)}, bf16[2,8,4,128]{3,2,1,0:T(4,128)(2,1)S(1)}, u32[]{:S(2)}, u32[]{:S(2)}) %collective-permute-start) | collective-permute-done | bytes 16416 | tf_op jit(solution)/shard_map/ppermute | solution.py:534
  1.5 0.3 %copy-done = bf16[2,8,4,128]{3,2,1,0:T(4,128)(2,1)S(1)} copy-done((bf16[2,8,4,128]{3,2,1,0:T(4,128)(2,1)S(1)}, bf16[2,8,4,128]{3,2,1,0:T(4,128)(2,1)}, u32[]{:S(2)}) %copy-start) | copy-done | bytes 16408
  1.9 2.6 %collective-permute-start.1 = (bf16[8,768]{1,0:T(8,128)(2,1)S(1)}, bf16[8,768]{1,0:T(8,128)(2,1)S(1)}, u32[]{:S(2)}, u32[]{:S(2)}) collective-permute-start(bf16[8,768]{1,0:T(8,128)(2,1)S(1)} %six_rows.1.mine_ref), channel_id=1, source_target_pairs={{0,16},{1,2},{2,1},{3,4},{4,3},{5,6},{6,5},{7,8},{8,7},{9,10},{10,... | collective-permute-start | bytes 36872 | tf_op jit(solution)/shard_map/ppermute | solution.py:534
  4.5 0.0 copy-done.4
  4.5 0.0 copy-start.7
  4.5 0.3 %weights.1 = (bf16[192,72]{1,0:T(8,128)(2,1)S(1)}, bf16[2,192,1728]{2,1,0:T(8,128)(2,1)S(1)}, bf16[256,144]{1,0:T(8,128)(2,1)S(1)}, bf16[256,192]{1,0:T(8,128)(2,1)S(1)}) custom-call(f32[256,128]{1,0:T(8,128)S(1)} %prepare.1.embed_ref, bf16[72,192]{1,0:T(8,128)(2,1)S(1)} %bitcast.6, bf16[2,192,1728]{2,1,0:T(8,128)(2,1)S(1)} %copy-done.1, ...), custom_call_target="tpu_custom_call" | custom-call | flops 4000000000 | tf_op jit(solution)/shard_map/weights/pallas_call | solution.py:556
  4.8 1.3 %collective-permute-done.1.across_ref = bf16[8,768]{1,0:T(8,128)(2,1)S(1)} collective-permute-done((bf16[8,768]{1,0:T(8,128)(2,1)S(1)}, bf16[8,768]{1,0:T(8,128)(2,1)S(1)}, u32[]{:S(2)}, u32[]{:S(2)}) %collective-permute-start.1) | collective-permute-done | bytes 12320 | tf_op jit(solution)/shard_map/ppermute | solution.py:534
  6.1 0.0 copy-done.7
  6.1 4.2 %regress.1 = (f32[8,1024]{1,0:T(8,128)S(1)}, bf16[192,512]{1,0:T(8,128)(2,1)S(1)}, f32[4,1024]{1,0:T(4,128)S(1)}, bf16[208,256]{1,0:T(8,128)(2,1)S(1)}, f32[192,...) custom-call(bf16[8,768]{1,0:T(8,128)(2,1)S(1)} %six_rows.1.mine_ref,, ...), custom_call_target="tpu_custom_call" | custom-call | flops 3000000000 | tf_op jit(solution)/shard_map/regress/pallas_call | solution.py:565
  10.4 0.1 collective-permute-start.2
  10.5 1.3 %outer.1 = (bf16[192,256]{1,0:T(8,128)(2,1)S(1)}, f32[4,512]{1,0:T(4,128)S(1)}) custom-call(bf16[2,192,1728]{2,1,0:T(8,128)(2,1)S(1)} %get-tuple-element.42.reg_mid_ref, bf16[4,192]{1,0:T(4,128)(2,1)S(1)} %copy-done.7, f32[192,256]{1,0:T(8,128)S(1)} %get-tuple-element.47.refs_0_, f32[192,256]{1,0:T(8,128)S(1)} %get-tuple-element.48.refs_1_, ...), custom_call_target="tpu_custom_call" | custom-call | flops 1000000000 | tf_op jit(solution)/shard_map/outer/pallas_call | solution.py:579
  11.7 0.0 collective-permute-done.2.pair_ref
  11.8 0.0 copy-done.6
  11.8 5.1 %denoise.1 = (f32[4,512]{1,0:T(4,128)S(1)}, f32[4,512]{1,0:T(4,128)S(1)}, f32[4,256]{1,0:T(4,128)S(1)}, f32[4,256]{1,0:T(4,128)S(1)}) custom-call(f32[8,1024]{1,0:T(8,128)S(1)} %get-tuple-element.43.rows_ref, f32[2,4,8,128]{3,2,1,0:T(8,128)S(1)} %copy-done.6, bf16[192,512]{1,0:T(8,128)(2,1)S(1)} %get-tuple-element.44.skip_ref, ...), custom_call_target="tpu_custom_call" | custom-call | flops 4000000000 | tf_op jit(solution)/shard_map/denoise/pallas_call | solution.py:586
  16.9 0.4 %collective-permute-start.3 = (f32[4,256]{1,0:T(4,128)S(1)}, f32[4,256]{1,0:T(4,128)S(1)}, u32[]{:S(2)}, u32[]{:S(2)}) collective-permute-start(f32[4,256]{1,0:T(4,128)S(1)} %get-tuple-element.73), channel_id=1, source_target_pairs={{0,1},{1,0},{2,3},{3,2},{4,5},{5,4},{6,7},{7,6},{8,9},{9,8},{10,11... | collective-permute-start | bytes 12296 | tf_op jit(solution)/shard_map/ppermute | solution.py:534
  17.3 2.0 %collective-permute-start.4 = (f32[4,256]{1,0:T(4,128)S(1)}, f32[4,256]{1,0:T(4,128)S(1)}, u32[]{:S(2)}, u32[]{:S(2)}) collective-permute-start(f32[4,256]{1,0:T(4,128)S(1)} %get-tuple-element.74), channel_id=1, source_target_pairs={{0,16},{1,2},{2,1},{3,4},{4,3},{5,6},{6,5},{7,8},{8,7},{9,10},{10,... | collective-permute-start | bytes 12296 | tf_op jit(solution)/shard_map/ppermute | solution.py:534
  19.4 0.0 collective-permute-done.3.pair_ref
  19.4 1.6 %collective-permute-done.4.next_ref = f32[4,256]{1,0:T(4,128)S(1)} collective-permute-done((f32[4,256]{1,0:T(4,128)S(1)}, f32[4,256]{1,0:T(4,128)S(1)}, u32[]{:S(2)}, u32[]{:S(2)}) %collective-permute-start.4) | collective-permute-done | bytes 4128 | tf_op jit(solution)/shard_map/ppermute | solution.py:534
  21.0 2.1 %collective-permute-start.5 = (f32[4,4,128]{2,1,0:T(4,128)S(1)}, f32[4,4,128]{2,1,0:T(4,128)S(1)}, u32[]{:S(2)}, u32[]{:S(2)}) collective-permute-start(f32[4,4,128]{2,1,0:T(4,128)S(1)} %get-tuple-element.76), channel_id=1, source_target_pairs={{0,16},{1,17},{2,18},{3,19},{4,20},{5,21},{6,22},{7,23},{8,24},{9,... | collective-permute-start | bytes 24584 | tf_op jit(solution)/shard_map/ppermute | solution.py:534
  23.0 1.6 %collective-permute-done.5.got_ref = f32[4,4,128]{2,1,0:T(4,128)S(1)} collective-permute-done((f32[4,4,128]{2,1,0:T(4,128)S(1)}, f32[4,4,128]{2,1,0:T(4,128)S(1)}, u32[]{:S(2)}, u32[]{:S(2)}) %collective-permute-start.5) | collective-permute-done | bytes 8224 | tf_op jit(solution)/shard_map/ppermute | solution.py:534
  24.7 0.6 %output.1 = f32[1,2,4,4,128]{4,3,2,1,0:T(4,128)} custom-call(f32[4,4,128]{2,1,0:T(4,128)S(1)} %get-tuple-element.75.own_ref, f32[4,4,128]{2,1,0:T(4,128)S(1)} %collective-permute-done.5.got_ref), custom_call_target="tpu_custom_call" | custom-call | tf_op jit(solution)/shard_map/output/pallas_call | solution.py:612
  (17 shorter events, 0.1 us)
Async XLA Ops:
  0.0 1.5 %collective-permute-start = (bf16[2,8,4,128]{3,2,1,0:T(4,128)(2,1)}, bf16[2,8,4,128]{3,2,1,0:T(4,128)(2,1)S(1)}, u32[]{:S(2)}, u32[]{:S(2)}) collective-permute-start(bf16[2,8,4,128]{3,2,1,0:T(4,128)(2,1)} %coarse_ref.1), channel_id=1, source_target_pairs={{0,1},{1,0},{2,3},{3,2},{4,5},{5,4},{6,7},{7,6},{8,9},{9,8},{10,11... | collective-permute-start | bytes 49160 | tf_op jit(solution)/shard_map/ppermute | solution.py:534
  0.5 0.7 %copy-start.9 = (f32[256]{0:T(256)S(1)}, f32[256]{0:T(256)}, u32[]{:S(2)}) copy-start(f32[256]{0:T(256)} %param.19) | copy-start | bytes 3076
  1.1 0.7 %copy-start = (bf16[2,8,4,128]{3,2,1,0:T(4,128)(2,1)S(1)}, bf16[2,8,4,128]{3,2,1,0:T(4,128)(2,1)}, u32[]{:S(2)}) copy-start(bf16[2,8,4,128]{3,2,1,0:T(4,128)(2,1)} %coarse_ref.1) | copy-start | bytes 49156
  1.1 3.3 %copy-start.1 = (bf16[2,192,1728]{2,1,0:T(8,128)(2,1)S(1)}, bf16[2,192,1728]{2,1,0:T(8,128)(2,1)}, u32[]{:S(2)}) copy-start(bf16[2,192,1728]{2,1,0:T(8,128)(2,1)} %reg_mid_ref.1) | copy-start | bytes 3981316
  1.1 3.3 %copy-start.3 = (bf16[256,192]{0,1:T(8,128)(2,1)S(1)}, bf16[256,192]{0,1:T(8,128)(2,1)}, u32[]{:S(2)}) copy-start(bf16[256,192]{0,1:T(8,128)(2,1)} %param.16) | copy-start | bytes 294916
  1.1 3.3 %copy-start.4 = (bf16[256,144]{0,1:T(8,128)(2,1)S(1)}, bf16[256,144]{0,1:T(8,128)(2,1)}, u32[]{:S(2)}) copy-start(bf16[256,144]{0,1:T(8,128)(2,1)} %param.15) | copy-start | bytes 221188
  1.1 3.3 %copy-start.5 = (bf16[192,72]{0,1:T(8,128)(2,1)S(1)}, bf16[192,72]{0,1:T(8,128)(2,1)}, u32[]{:S(2)}) copy-start(bf16[192,72]{0,1:T(8,128)(2,1)} %param.12) | copy-start | bytes 82948
  1.9 4.3 %collective-permute-start.1 = (bf16[8,768]{1,0:T(8,128)(2,1)S(1)}, bf16[8,768]{1,0:T(8,128)(2,1)S(1)}, u32[]{:S(2)}, u32[]{:S(2)}) collective-permute-start(bf16[8,768]{1,0:T(8,128)(2,1)S(1)} %six_rows.1.mine_ref), channel_id=1, source_target_pairs={{0,16},{1,2},{2,1},{3,4},{4,3},{5,6},{6,5},{7,8},{8,7},{9,10},{10,... | collective-permute-start | bytes 36872 | tf_op jit(solution)/shard_map/ppermute | solution.py:534
  4.5 1.7 %copy-start.7 = (bf16[4,192]{1,0:T(4,128)(2,1)S(1)}, bf16[4,192]{1,0:T(4,128)(2,1)}, u32[]{:S(2)}) copy-start(bf16[4,192]{1,0:T(4,128)(2,1)} %reg_out_ref.3) | copy-start | bytes 4612
  10.4 1.4 %collective-permute-start.2 = (bf16[208,256]{1,0:T(8,128)(2,1)S(1)}, bf16[208,256]{1,0:T(8,128)(2,1)S(1)}, u32[]{:S(2)}, u32[]{:S(2)}) collective-permute-start(bf16[208,256]{1,0:T(8,128)(2,1)S(1)} %get-tuple-element.46), channel_id=1, source_target_pairs={{0,1},{1,0},{2,3},{3,2},{4,5},{5,4},{6,7},{7,6},{8,9},{9,8},{10,11... | collective-permute-start | bytes 319496 | tf_op jit(solution)/shard_map/ppermute | solution.py:534
  10.5 1.3 %copy-start.2 = (bf16[256,2304]{1,0:T(8,128)(2,1)S(1)}, bf16[256,2304]{1,0:T(8,128)(2,1)}, u32[]{:S(2)}) copy-start(bf16[256,2304]{1,0:T(8,128)(2,1)} %diff_mid_ref.1) | copy-start | bytes 3538948
  10.5 1.3 %copy-start.6 = (f32[2,4,8,128]{3,2,1,0:T(8,128)S(1)}, f32[2,4,8,128]{3,2,1,0:T(8,128)}, u32[]{:S(2)}) copy-start(f32[2,4,8,128]{3,2,1,0:T(8,128)} %noise_ref.1) | copy-start | bytes 98308
  10.5 1.3 %copy-start.8 = (bf16[4,256]{1,0:T(4,128)(2,1)S(1)}, bf16[4,256]{1,0:T(4,128)(2,1)}, u32[]{:S(2)}) copy-start(bf16[4,256]{1,0:T(4,128)(2,1)} %diff_out_ref.1) | copy-start | bytes 6148
  16.9 2.4 %collective-permute-start.3 = (f32[4,256]{1,0:T(4,128)S(1)}, f32[4,256]{1,0:T(4,128)S(1)}, u32[]{:S(2)}, u32[]{:S(2)}) collective-permute-start(f32[4,256]{1,0:T(4,128)S(1)} %get-tuple-element.73), channel_id=1, source_target_pairs={{0,1},{1,0},{2,3},{3,2},{4,5},{5,4},{6,7},{7,6},{8,9},{9,8},{10,11... | collective-permute-start | bytes 12296 | tf_op jit(solution)/shard_map/ppermute | solution.py:534
  17.3 3.6 %collective-permute-start.4 = (f32[4,256]{1,0:T(4,128)S(1)}, f32[4,256]{1,0:T(4,128)S(1)}, u32[]{:S(2)}, u32[]{:S(2)}) collective-permute-start(f32[4,256]{1,0:T(4,128)S(1)} %get-tuple-element.74), channel_id=1, source_target_pairs={{0,16},{1,2},{2,1},{3,4},{4,3},{5,6},{6,5},{7,8},{8,7},{9,10},{10,... | collective-permute-start | bytes 12296 | tf_op jit(solution)/shard_map/ppermute | solution.py:534
  21.0 3.7 %collective-permute-start.5 = (f32[4,4,128]{2,1,0:T(4,128)S(1)}, f32[4,4,128]{2,1,0:T(4,128)S(1)}, u32[]{:S(2)}, u32[]{:S(2)}) collective-permute-start(f32[4,4,128]{2,1,0:T(4,128)S(1)} %get-tuple-element.76), channel_id=1, source_target_pairs={{0,16},{1,17},{2,18},{3,19},{4,20},{5,21},{6,22},{7,23},{8,24},{9,... | collective-permute-start | bytes 24584 | tf_op jit(solution)/shard_map/ppermute | solution.py:534

commit v5 on v4

--- a/solution.py
+++ b/solution.py
@@ -453,10 +453,11 @@
             return fresh + base[outs, lanes(r, STEP)] + shift[outs]
 
         run(patch.start_steps(0, first_rows))
-        run(patch.start_steps(1, first_rows))
-        run(patch.act_steps(0))
-        run(patch.act_steps(1))
-        run(patch.first_steps(diff_mid_ref))
+        run(patch.act_steps(0), patch.start_steps(1, first_rows))
+        acts = patch.act_steps(1)
+        for k, step in enumerate(patch.first_steps(diff_mid_ref)):
+            run(acts[k * STEP : (k + 1) * STEP])
+            step()
         run(patch.last_steps(diff_mid_ref, 0))
         run(patch.last_steps(diff_mid_ref, 1))
         scales = [[jnp.concatenate([s] * STEP, axis=1) for s in part] for part in patch.scales]

time: 25.5 us -> 25.5 us (level)
  no operation moved by 1% of the time
where the time goes in v5:
time: 25.5 us; the launch traced here: 25.3 us
  Pallas kernels  11.7 us (46%)
  starting transfers between devices  7.67 us (30%)
  waiting for transfers between devices  4.8 us (19%)
  local copies, waits for them, and re-layouts  1.06 us (4%)
    ppermute x6, starting transfers between devices, permute(): return lax.ppermute(value, ('segment', 'tile'), edges)  7.67 us
    pallas_call x1, Pallas kernels, shards(): call(denoise_kernel, 'denoise', [((fields, band_cells), F32), ((fields, b...  5.14 us
    ppermute x6, waiting for transfers between devices, permute(): return lax.ppermute(value, ('segment', 'tile'), edges)  4.8 us
    pallas_call x1, Pallas kernels, shards(): call(regress_kernel, 'regress', [((inputs, cells), F32), ((width_r, band_...  4.21 us
    pallas_call x1, Pallas kernels, shards(): call(outer_kernel, 'outer', [((width_r, edge_cells), BF16), ((fields, ban...  1.27 us
    unnamed x20, local copies, waits for them, and re-layouts  1.06 us
    pallas_call x1, Pallas kernels, shards(): call(output_kernel, 'output', [((1, 2, fields, BAND, LANES), F32)])  0.61 us
  transfers between devices with their start and end apart: 6, of which 4 were waited for; matrix products, arithmetic and copies ran while one was open for 0% of the time, Pallas kernels for 7%

profile of v5, /device:TPU:0, one launch (start us, length us, event | category | flops | bytes accessed | tf_op | source)
XLA Modules:
  0.0 25.3 jit_solution(11630165604568489950)
XLA Ops:
  0.0 0.5 %collective-permute-start = (bf16[2,8,4,128]{3,2,1,0:T(4,128)(2,1)}, bf16[2,8,4,128]{3,2,1,0:T(4,128)(2,1)S(1)}, u32[]{:S(2)}, u32[]{:S(2)}) collective-permute-start(bf16[2,8,4,128]{3,2,1,0:T(4,128)(2,1)} %coarse_ref.1), channel_id=1, source_target_pairs={{0,1},{1,0},{2,3},{3,2},{4,5},{5,4},{6,7},{7,6},{8,9},{9,8},{10,11... | collective-permute-start | bytes 49160 | tf_op jit(solution)/shard_map/ppermute | solution.py:535
  0.5 0.7 %copy-done.9 = f32[256]{0:T(256)S(1)} copy-done((f32[256]{0:T(256)S(1)}, f32[256]{0:T(256)}, u32[]{:S(2)}) %copy-start.9) | copy-done | bytes 1048
  1.2 0.1 prepare.1.embed_ref
  1.2 0.3 %collective-permute-done.pair_ref = bf16[2,8,4,128]{3,2,1,0:T(4,128)(2,1)S(1)} collective-permute-done((bf16[2,8,4,128]{3,2,1,0:T(4,128)(2,1)}, bf16[2,8,4,128]{3,2,1,0:T(4,128)(2,1)S(1)}, u32[]{:S(2)}, u32[]{:S(2)}) %collective-permute-start) | collective-permute-done | bytes 16416 | tf_op jit(solution)/shard_map/ppermute | solution.py:535
  1.5 0.3 %copy-done = bf16[2,8,4,128]{3,2,1,0:T(4,128)(2,1)S(1)} copy-done((bf16[2,8,4,128]{3,2,1,0:T(4,128)(2,1)S(1)}, bf16[2,8,4,128]{3,2,1,0:T(4,128)(2,1)}, u32[]{:S(2)}) %copy-start) | copy-done | bytes 16408
  1.9 2.6 %collective-permute-start.1 = (bf16[8,768]{1,0:T(8,128)(2,1)S(1)}, bf16[8,768]{1,0:T(8,128)(2,1)S(1)}, u32[]{:S(2)}, u32[]{:S(2)}) collective-permute-start(bf16[8,768]{1,0:T(8,128)(2,1)S(1)} %six_rows.1.mine_ref), channel_id=1, source_target_pairs={{0,16},{1,2},{2,1},{3,4},{4,3},{5,6},{6,5},{7,8},{8,7},{9,10},{10,... | collective-permute-start | bytes 36872 | tf_op jit(solution)/shard_map/ppermute | solution.py:535
  4.5 0.0 copy-done.4
  4.5 0.0 copy-start.7
  4.5 0.3 %weights.1 = (bf16[192,72]{1,0:T(8,128)(2,1)S(1)}, bf16[2,192,1728]{2,1,0:T(8,128)(2,1)S(1)}, bf16[256,144]{1,0:T(8,128)(2,1)S(1)}, bf16[256,192]{1,0:T(8,128)(2,1)S(1)}) custom-call(f32[256,128]{1,0:T(8,128)S(1)} %prepare.1.embed_ref, bf16[72,192]{1,0:T(8,128)(2,1)S(1)} %bitcast.6, bf16[2,192,1728]{2,1,0:T(8,128)(2,1)S(1)} %copy-done.1, ...), custom_call_target="tpu_custom_call" | custom-call | flops 4000000000 | tf_op jit(solution)/shard_map/weights/pallas_call | solution.py:557
  4.8 1.3 %collective-permute-done.1.across_ref = bf16[8,768]{1,0:T(8,128)(2,1)S(1)} collective-permute-done((bf16[8,768]{1,0:T(8,128)(2,1)S(1)}, bf16[8,768]{1,0:T(8,128)(2,1)S(1)}, u32[]{:S(2)}, u32[]{:S(2)}) %collective-permute-start.1) | collective-permute-done | bytes 12320 | tf_op jit(solution)/shard_map/ppermute | solution.py:535
  6.1 0.0 copy-done.7
  6.1 4.2 %regress.1 = (f32[8,1024]{1,0:T(8,128)S(1)}, bf16[192,512]{1,0:T(8,128)(2,1)S(1)}, f32[4,1024]{1,0:T(4,128)S(1)}, bf16[208,256]{1,0:T(8,128)(2,1)S(1)}, f32[192,...) custom-call(bf16[8,768]{1,0:T(8,128)(2,1)S(1)} %six_rows.1.mine_ref,, ...), custom_call_target="tpu_custom_call" | custom-call | flops 3000000000 | tf_op jit(solution)/shard_map/regress/pallas_call | solution.py:566
  10.4 0.1 collective-permute-start.2
  10.5 1.3 %outer.1 = (bf16[192,256]{1,0:T(8,128)(2,1)S(1)}, f32[4,512]{1,0:T(4,128)S(1)}) custom-call(bf16[2,192,1728]{2,1,0:T(8,128)(2,1)S(1)} %get-tuple-element.42.reg_mid_ref, bf16[4,192]{1,0:T(4,128)(2,1)S(1)} %copy-done.7, f32[192,256]{1,0:T(8,128)S(1)} %get-tuple-element.47.refs_0_, f32[192,256]{1,0:T(8,128)S(1)} %get-tuple-element.48.refs_1_, ...), custom_call_target="tpu_custom_call" | custom-call | flops 1000000000 | tf_op jit(solution)/shard_map/outer/pallas_call | solution.py:580
  11.7 0.0 collective-permute-done.2.pair_ref
  11.8 0.0 copy-done.6
  11.8 5.1 %denoise.1 = (f32[4,512]{1,0:T(4,128)S(1)}, f32[4,512]{1,0:T(4,128)S(1)}, f32[4,256]{1,0:T(4,128)S(1)}, f32[4,256]{1,0:T(4,128)S(1)}) custom-call(f32[8,1024]{1,0:T(8,128)S(1)} %get-tuple-element.43.rows_ref, f32[2,4,8,128]{3,2,1,0:T(8,128)S(1)} %copy-done.6, bf16[192,512]{1,0:T(8,128)(2,1)S(1)} %get-tuple-element.44.skip_ref, ...), custom_call_target="tpu_custom_call" | custom-call | flops 4000000000 | tf_op jit(solution)/shard_map/denoise/pallas_call | solution.py:587
  16.9 0.4 %collective-permute-start.3 = (f32[4,256]{1,0:T(4,128)S(1)}, f32[4,256]{1,0:T(4,128)S(1)}, u32[]{:S(2)}, u32[]{:S(2)}) collective-permute-start(f32[4,256]{1,0:T(4,128)S(1)} %get-tuple-element.73), channel_id=1, source_target_pairs={{0,1},{1,0},{2,3},{3,2},{4,5},{5,4},{6,7},{7,6},{8,9},{9,8},{10,11... | collective-permute-start | bytes 12296 | tf_op jit(solution)/shard_map/ppermute | solution.py:535
  17.3 2.0 %collective-permute-start.4 = (f32[4,256]{1,0:T(4,128)S(1)}, f32[4,256]{1,0:T(4,128)S(1)}, u32[]{:S(2)}, u32[]{:S(2)}) collective-permute-start(f32[4,256]{1,0:T(4,128)S(1)} %get-tuple-element.74), channel_id=1, source_target_pairs={{0,16},{1,2},{2,1},{3,4},{4,3},{5,6},{6,5},{7,8},{8,7},{9,10},{10,... | collective-permute-start | bytes 12296 | tf_op jit(solution)/shard_map/ppermute | solution.py:535
  19.4 0.0 collective-permute-done.3.pair_ref
  19.4 1.6 %collective-permute-done.4.next_ref = f32[4,256]{1,0:T(4,128)S(1)} collective-permute-done((f32[4,256]{1,0:T(4,128)S(1)}, f32[4,256]{1,0:T(4,128)S(1)}, u32[]{:S(2)}, u32[]{:S(2)}) %collective-permute-start.4) | collective-permute-done | bytes 4128 | tf_op jit(solution)/shard_map/ppermute | solution.py:535
  21.0 2.1 %collective-permute-start.5 = (f32[4,4,128]{2,1,0:T(4,128)S(1)}, f32[4,4,128]{2,1,0:T(4,128)S(1)}, u32[]{:S(2)}, u32[]{:S(2)}) collective-permute-start(f32[4,4,128]{2,1,0:T(4,128)S(1)} %get-tuple-element.76), channel_id=1, source_target_pairs={{0,16},{1,17},{2,18},{3,19},{4,20},{5,21},{6,22},{7,23},{8,24},{9,... | collective-permute-start | bytes 24584 | tf_op jit(solution)/shard_map/ppermute | solution.py:535
  23.0 1.6 %collective-permute-done.5.got_ref = f32[4,4,128]{2,1,0:T(4,128)S(1)} collective-permute-done((f32[4,4,128]{2,1,0:T(4,128)S(1)}, f32[4,4,128]{2,1,0:T(4,128)S(1)}, u32[]{:S(2)}, u32[]{:S(2)}) %collective-permute-start.5) | collective-permute-done | bytes 8224 | tf_op jit(solution)/shard_map/ppermute | solution.py:535
  24.7 0.6 %output.1 = f32[1,2,4,4,128]{4,3,2,1,0:T(4,128)} custom-call(f32[4,4,128]{2,1,0:T(4,128)S(1)} %get-tuple-element.75.own_ref, f32[4,4,128]{2,1,0:T(4,128)S(1)} %collective-permute-done.5.got_ref), custom_call_target="tpu_custom_call" | custom-call | tf_op jit(solution)/shard_map/output/pallas_call | solution.py:613
  (17 shorter events, 0.1 us)
Async XLA Ops:
  0.0 1.5 %collective-permute-start = (bf16[2,8,4,128]{3,2,1,0:T(4,128)(2,1)}, bf16[2,8,4,128]{3,2,1,0:T(4,128)(2,1)S(1)}, u32[]{:S(2)}, u32[]{:S(2)}) collective-permute-start(bf16[2,8,4,128]{3,2,1,0:T(4,128)(2,1)} %coarse_ref.1), channel_id=1, source_target_pairs={{0,1},{1,0},{2,3},{3,2},{4,5},{5,4},{6,7},{7,6},{8,9},{9,8},{10,11... | collective-permute-start | bytes 49160 | tf_op jit(solution)/shard_map/ppermute | solution.py:535
  0.5 0.7 %copy-start.9 = (f32[256]{0:T(256)S(1)}, f32[256]{0:T(256)}, u32[]{:S(2)}) copy-start(f32[256]{0:T(256)} %param.19) | copy-start | bytes 3076
  1.1 0.7 %copy-start = (bf16[2,8,4,128]{3,2,1,0:T(4,128)(2,1)S(1)}, bf16[2,8,4,128]{3,2,1,0:T(4,128)(2,1)}, u32[]{:S(2)}) copy-start(bf16[2,8,4,128]{3,2,1,0:T(4,128)(2,1)} %coarse_ref.1) | copy-start | bytes 49156
  1.1 3.3 %copy-start.1 = (bf16[2,192,1728]{2,1,0:T(8,128)(2,1)S(1)}, bf16[2,192,1728]{2,1,0:T(8,128)(2,1)}, u32[]{:S(2)}) copy-start(bf16[2,192,1728]{2,1,0:T(8,128)(2,1)} %reg_mid_ref.1) | copy-start | bytes 3981316
  1.1 3.3 %copy-start.3 = (bf16[256,192]{0,1:T(8,128)(2,1)S(1)}, bf16[256,192]{0,1:T(8,128)(2,1)}, u32[]{:S(2)}) copy-start(bf16[256,192]{0,1:T(8,128)(2,1)} %param.16) | copy-start | bytes 294916
  1.1 3.3 %copy-start.4 = (bf16[256,144]{0,1:T(8,128)(2,1)S(1)}, bf16[256,144]{0,1:T(8,128)(2,1)}, u32[]{:S(2)}) copy-start(bf16[256,144]{0,1:T(8,128)(2,1)} %param.15) | copy-start | bytes 221188
  1.1 3.3 %copy-start.5 = (bf16[192,72]{0,1:T(8,128)(2,1)S(1)}, bf16[192,72]{0,1:T(8,128)(2,1)}, u32[]{:S(2)}) copy-start(bf16[192,72]{0,1:T(8,128)(2,1)} %param.12) | copy-start | bytes 82948
  1.9 4.3 %collective-permute-start.1 = (bf16[8,768]{1,0:T(8,128)(2,1)S(1)}, bf16[8,768]{1,0:T(8,128)(2,1)S(1)}, u32[]{:S(2)}, u32[]{:S(2)}) collective-permute-start(bf16[8,768]{1,0:T(8,128)(2,1)S(1)} %six_rows.1.mine_ref), channel_id=1, source_target_pairs={{0,16},{1,2},{2,1},{3,4},{4,3},{5,6},{6,5},{7,8},{8,7},{9,10},{10,... | collective-permute-start | bytes 36872 | tf_op jit(solution)/shard_map/ppermute | solution.py:535
  4.5 1.7 %copy-start.7 = (bf16[4,192]{1,0:T(4,128)(2,1)S(1)}, bf16[4,192]{1,0:T(4,128)(2,1)}, u32[]{:S(2)}) copy-start(bf16[4,192]{1,0:T(4,128)(2,1)} %reg_out_ref.3) | copy-start | bytes 4612
  10.4 1.4 %collective-permute-start.2 = (bf16[208,256]{1,0:T(8,128)(2,1)S(1)}, bf16[208,256]{1,0:T(8,128)(2,1)S(1)}, u32[]{:S(2)}, u32[]{:S(2)}) collective-permute-start(bf16[208,256]{1,0:T(8,128)(2,1)S(1)} %get-tuple-element.46), channel_id=1, source_target_pairs={{0,1},{1,0},{2,3},{3,2},{4,5},{5,4},{6,7},{7,6},{8,9},{9,8},{10,11... | collective-permute-start | bytes 319496 | tf_op jit(solution)/shard_map/ppermute | solution.py:535
  10.5 1.3 %copy-start.2 = (bf16[256,2304]{1,0:T(8,128)(2,1)S(1)}, bf16[256,2304]{1,0:T(8,128)(2,1)}, u32[]{:S(2)}) copy-start(bf16[256,2304]{1,0:T(8,128)(2,1)} %diff_mid_ref.1) | copy-start | bytes 3538948
  10.5 1.3 %copy-start.6 = (f32[2,4,8,128]{3,2,1,0:T(8,128)S(1)}, f32[2,4,8,128]{3,2,1,0:T(8,128)}, u32[]{:S(2)}) copy-start(f32[2,4,8,128]{3,2,1,0:T(8,128)} %noise_ref.1) | copy-start | bytes 98308
  10.5 1.3 %copy-start.8 = (bf16[4,256]{1,0:T(4,128)(2,1)S(1)}, bf16[4,256]{1,0:T(4,128)(2,1)}, u32[]{:S(2)}) copy-start(bf16[4,256]{1,0:T(4,128)(2,1)} %diff_out_ref.1) | copy-start | bytes 6148
  16.9 2.4 %collective-permute-start.3 = (f32[4,256]{1,0:T(4,128)S(1)}, f32[4,256]{1,0:T(4,128)S(1)}, u32[]{:S(2)}, u32[]{:S(2)}) collective-permute-start(f32[4,256]{1,0:T(4,128)S(1)} %get-tuple-element.73), channel_id=1, source_target_pairs={{0,1},{1,0},{2,3},{3,2},{4,5},{5,4},{6,7},{7,6},{8,9},{9,8},{10,11... | collective-permute-start | bytes 12296 | tf_op jit(solution)/shard_map/ppermute | solution.py:535
  17.3 3.6 %collective-permute-start.4 = (f32[4,256]{1,0:T(4,128)S(1)}, f32[4,256]{1,0:T(4,128)S(1)}, u32[]{:S(2)}, u32[]{:S(2)}) collective-permute-start(f32[4,256]{1,0:T(4,128)S(1)} %get-tuple-element.74), channel_id=1, source_target_pairs={{0,16},{1,2},{2,1},{3,4},{4,3},{5,6},{6,5},{7,8},{8,7},{9,10},{10,... | collective-permute-start | bytes 12296 | tf_op jit(solution)/shard_map/ppermute | solution.py:535
  21.0 3.7 %collective-permute-start.5 = (f32[4,4,128]{2,1,0:T(4,128)S(1)}, f32[4,4,128]{2,1,0:T(4,128)S(1)}, u32[]{:S(2)}, u32[]{:S(2)}) collective-permute-start(f32[4,4,128]{2,1,0:T(4,128)S(1)} %get-tuple-element.76), channel_id=1, source_target_pairs={{0,16},{1,17},{2,18},{3,19},{4,20},{5,21},{6,22},{7,23},{8,24},{9,... | collective-permute-start | bytes 24584 | tf_op jit(solution)/shard_map/ppermute | solution.py:535
